TPU v7x, 32 devices: a whole 2x2x4 slice. The times are simulated.
32 devices in a mesh: pb: 8 (over z, y), ka: 4 (over x, core).
Axes of the slice: x: 2, y: 2, z: 4, core: 2. Of those that a mesh axis runs over, the one named last changes fastest.
Arguments:
- queries: bfloat16 [2048, 4096], P('pb', 'ka'), may hold values from -25 to 25
- output_gradient: bfloat16 [2048, 4096], P('pb', 'ka'), may hold values from -6 to 6
- key_states: bfloat16 [2048, 2048], P(('pb', 'ka')), may hold values from -6 to 6
- value_inputs: bfloat16 [2048, 2048], P(('pb', 'ka')), may hold values from -6 to 6
- turn_ids: int32 [2048], replicated, may hold values from 0 to 3, never falling along the last dimension, each value on 1 to 1792 neighbouring positions
- listed: int32 [2, 16, 14], replicated, may hold values 0 or 1
Outputs:
- grad_queries: float32 [2048, 4096], P('pb', 'ka')
- grad_keys: float32 [2048, 2048], P(('pb', 'ka'))
- grad_values: float32 [2048, 2048], P(('pb', 'ka'))
Inputs may be any that keep to these rules, and one draw needn't show every extreme that they name: `turn_ids`: turn numbers never fall along the window; every turn spans 1 to 1792 positions, and some turn spans exactly 1792.
All inputs are finite; a program needn't handle non-finite values.
Results may differ from a plain program's by a relative error of at most 0.003.
Values may be sent and summed in bfloat16 or wider, within the bound.
A program may use at most 128 MiB of HBM per device.

v0:
```python
import jax
import jax.numpy as jnp
from jax import lax
from jax.sharding import PartitionSpec as P

QUERY_HEADS = 32
KEY_VALUE_HEADS = 16
HEAD_SIZE = 128
HEAD_GROUPS = 2
BLOCK_POSITIONS = 128
BACK = 14


SCORE_SCALE = 1.0 / 12.0
NEG_LARGE = -1e30


def shifted(x, axis, by):
    count = lax.axis_size(axis)
    pairs = [(i, i + by) for i in range(count) if 0 <= i + by < count]
    return lax.ppermute(x, axis, pairs)


def combined_all(x, axis, combine):
    everything = jax.tree.map(lambda part: lax.all_gather(part, axis), x)
    first = jax.tree.map(lambda part: part[0], everything)

    def hop(k, so_far):
        return combine(so_far, jax.tree.map(lambda part: part[k], everything))

    return lax.fori_loop(1, lax.axis_size(axis), hop, first)


def visible_mask(turn_ids, listed, query_begin, key_pos, tok_rows):
    query_pos = query_begin + jnp.arange(tok_rows, dtype=jnp.int32)
    query_turn = lax.dynamic_slice_in_dim(turn_ids, query_begin, tok_rows, 0)
    key_turn = turn_ids[jnp.clip(key_pos, 0, turn_ids.shape[0] - 1)]
    blk_count = tok_rows // BLOCK_POSITIONS
    query_blocks = query_begin // BLOCK_POSITIONS + jnp.arange(blk_count, dtype=jnp.int32)
    list_table = lax.dynamic_slice_in_dim(listed, query_begin // BLOCK_POSITIONS, blk_count, 1)
    offsets = query_blocks[:, None] - key_pos[None, :] // BLOCK_POSITIONS - 1
    onehot = (offsets[:, :, None] == jnp.arange(BACK, dtype=jnp.int32)[None, None, :]).astype(
        jnp.float32
    )
    listed_hit = jnp.einsum("gbo,bko->gbk", list_table.astype(jnp.float32), onehot) > 0.5
    listed_hit = jnp.repeat(listed_hit, BLOCK_POSITIONS, axis=1)
    causal_ok = (key_pos[None, :] <= query_pos[:, None]) & (key_pos[None, :] >= 0)
    same_turn = query_turn[:, None] == key_turn[None, :]
    return causal_ok[None] & (same_turn[None] | listed_hit)


def combine_terms(earlier_terms, later_terms):
    peak_max = jnp.maximum(earlier_terms[0], later_terms[0])
    first_factor = jnp.exp(earlier_terms[0] - peak_max)
    second_factor = jnp.exp(later_terms[0] - peak_max)
    return (
        peak_max,
        earlier_terms[1] * first_factor + later_terms[1] * second_factor,
        earlier_terms[2] * first_factor + later_terms[2] * second_factor,
    )


def fetch_window(stacked, win_depth):
    received = [stacked]
    moving = stacked
    for offset_dev in range(1, win_depth):
        moving = shifted(moving, "pb", 1)
        received.append(moving)
    return jnp.concatenate(received[::-1], axis=1)


def send_back(key_gradient, value_gradient, piece_rows, win_depth):

    def part_of(offset_dev):
        column = (win_depth - 1 - offset_dev) * piece_rows
        return jnp.stack(
            [
                key_gradient[column : column + piece_rows],
                value_gradient[column : column + piece_rows],
            ]
        )

    total_grad = part_of(0)
    for offset_dev in range(1, win_depth):
        total_grad = total_grad + shifted(part_of(offset_dev), "pb", -offset_dev)
    return total_grad


def per_device(queries, output_gradient, key_states, value_inputs, turn_ids, listed):
    tok_rows = queries.shape[0]
    win_depth = (BACK * BLOCK_POSITIONS + tok_rows - 1) // tok_rows + 1
    group_width = QUERY_HEADS // KEY_VALUE_HEADS
    head_cols = group_width * HEAD_SIZE
    group_head_count = KEY_VALUE_HEADS // HEAD_GROUPS
    pb_index = lax.axis_index("pb")
    ka_index = lax.axis_index("ka")
    piece_rows = key_states.shape[0]
    full_q, full_grad = (
        lax.all_gather(queries, "ka", axis=1, tiled=True),
        lax.all_gather(output_gradient, "ka", axis=1, tiled=True),
    )
    window = fetch_window(jnp.stack([key_states, value_inputs]), win_depth)
    key_total = win_depth * piece_rows
    column_ids = jnp.arange(key_total, dtype=jnp.int32)
    key_pos = (
        (pb_index - (win_depth - 1) + column_ids // piece_rows) * tok_rows
        + ka_index * piece_rows
        + column_ids % piece_rows
    )
    masks_all = visible_mask(turn_ids, listed, pb_index * tok_rows, key_pos, tok_rows)

    def scores_for(kv_head):
        query_cols = lax.dynamic_slice_in_dim(full_q, kv_head * head_cols, head_cols, 1).reshape(
            tok_rows, group_width, HEAD_SIZE
        )
        grad_cols = lax.dynamic_slice_in_dim(full_grad, kv_head * head_cols, head_cols, 1).reshape(
            tok_rows, group_width, HEAD_SIZE
        )
        key_head = lax.dynamic_slice_in_dim(window[0], kv_head * HEAD_SIZE, HEAD_SIZE, 1)
        value_head = lax.dynamic_slice_in_dim(window[1], kv_head * HEAD_SIZE, HEAD_SIZE, 1)
        allowed = lax.dynamic_index_in_dim(
            masks_all, kv_head // group_head_count, 0, keepdims=False
        )[None]
        raw_scores = (
            jnp.einsum("rqd,kd->qrk", query_cols, key_head, preferred_element_type=jnp.float32)
            * SCORE_SCALE
        )
        scores = jnp.where(allowed, raw_scores, NEG_LARGE)
        grad_prob = jnp.einsum(
            "rqd,kd->qrk", grad_cols, value_head, preferred_element_type=jnp.float32
        )
        return (query_cols, grad_cols, key_head, allowed, scores, grad_prob)

    def opening_sweep(kv_head, running):
        row_max, row_sum, row_dot = running
        query_cols, grad_cols, key_head, allowed, scores, grad_prob = scores_for(kv_head)
        local_max = jnp.max(scores, axis=2)
        weights = jnp.where(allowed, jnp.exp(scores - local_max[:, :, None]), 0.0)
        row_max = lax.dynamic_update_slice_in_dim(row_max, local_max, kv_head * group_width, 0)
        row_sum = lax.dynamic_update_slice_in_dim(
            row_sum, jnp.sum(weights, axis=2), kv_head * group_width, 0
        )
        row_dot = lax.dynamic_update_slice_in_dim(
            row_dot, jnp.sum(weights * grad_prob, axis=2), kv_head * group_width, 0
        )
        return (row_max, row_sum, row_dot)

    initial_terms = (
        jnp.full((QUERY_HEADS, tok_rows), NEG_LARGE, jnp.float32),
        jnp.zeros((QUERY_HEADS, tok_rows), jnp.float32),
        jnp.zeros((QUERY_HEADS, tok_rows), jnp.float32),
    )
    nearby_terms = lax.fori_loop(0, KEY_VALUE_HEADS, opening_sweep, initial_terms)
    peak_all, total_all, dot_all = combined_all(nearby_terms, "ka", combine_terms)
    delta_all = dot_all / total_all

    def closing_sweep(kv_head, running):
        query_gradient, key_gradient, value_gradient = running
        query_cols, grad_cols, key_head, allowed, scores, grad_prob = scores_for(kv_head)
        peak_max = lax.dynamic_slice_in_dim(peak_all, kv_head * group_width, group_width, 0)[
            :, :, None
        ]
        total_sum = lax.dynamic_slice_in_dim(total_all, kv_head * group_width, group_width, 0)[
            :, :, None
        ]
        delta_row = lax.dynamic_slice_in_dim(delta_all, kv_head * group_width, group_width, 0)[
            :, :, None
        ]
        soft_prob = jnp.where(allowed, jnp.exp(scores - peak_max), 0.0) / total_sum
        blended_rows = (SCORE_SCALE * soft_prob * (grad_prob - delta_row)).astype(jnp.bfloat16)
        probability_floor = soft_prob.astype(jnp.bfloat16)
        grad_q_head = jnp.einsum(
            "qrk,kd->rqd", blended_rows, key_head, preferred_element_type=jnp.float32
        ).reshape(tok_rows, head_cols)
        grad_k_head = jnp.einsum(
            "qrk,rqd->kd", blended_rows, query_cols, preferred_element_type=jnp.float32
        )
        grad_v_head = jnp.einsum(
            "qrk,rqd->kd", probability_floor, grad_cols, preferred_element_type=jnp.float32
        )
        query_gradient = lax.dynamic_update_slice_in_dim(
            query_gradient, grad_q_head, kv_head * head_cols, 1
        )
        key_gradient = lax.dynamic_update_slice_in_dim(
            key_gradient, grad_k_head, kv_head * HEAD_SIZE, 1
        )
        value_gradient = lax.dynamic_update_slice_in_dim(
            value_gradient, grad_v_head, kv_head * HEAD_SIZE, 1
        )
        return (query_gradient, key_gradient, value_gradient)

    initial_gradients = (
        jnp.zeros((tok_rows, QUERY_HEADS * HEAD_SIZE), jnp.float32),
        jnp.zeros((key_total, KEY_VALUE_HEADS * HEAD_SIZE), jnp.float32),
        jnp.zeros((key_total, KEY_VALUE_HEADS * HEAD_SIZE), jnp.float32),
    )
    query_gradient, key_gradient, value_gradient = lax.fori_loop(
        0, KEY_VALUE_HEADS, closing_sweep, initial_gradients
    )
    grad_queries = lax.psum_scatter(query_gradient, "ka", scatter_dimension=1, tiled=True)
    total_grad = send_back(key_gradient, value_gradient, piece_rows, win_depth)
    return (grad_queries, total_grad[0], total_grad[1])


def solution(mesh):
    in_specs = (
        P("pb", "ka"),
        P("pb", "ka"),
        P(("pb", "ka"), None),
        P(("pb", "ka"), None),
        P(),
        P(),
    )
    out_specs = (P("pb", "ka"), P(("pb", "ka"), None), P(("pb", "ka"), None))
    return jax.shard_map(
        per_device, mesh=mesh, in_specs=in_specs, out_specs=out_specs, check_vma=False
    )
```

profile of v0, /device:TPU:0, one launch (start us, length us, event | category | flops | bytes accessed | tf_op | source)
XLA Modules:
  0.0 557.9 jit_solution(6688153888846324920)
XLA Ops:
  10.4 4.9 collective-permute-start
  15.3 11.1 %collective-permute-done = bf16[2,64,2048]{2,1,0:T(8,128)(2,1)S(1)} collective-permute-done((bf16[2,64,2048]{2,1,0:T(8,128)(2,1)S(1)}, bf16[2,64,2048]{2,1,0:T(8,128)(2,1)S(1)}, u32[]{:S(2)}, u32[]{:S(2)}) %collective-permute-start) | collective-permute-done | bytes 524320 | tf_op jit(solution)/shard_map/ppermute | solution.py:21
  26.5 4.4 collective-permute-start.1
  30.9 10.4 %collective-permute-done.1 = bf16[2,64,2048]{2,1,0:T(8,128)(2,1)S(1)} collective-permute-done((bf16[2,64,2048]{2,1,0:T(8,128)(2,1)S(1)}, bf16[2,64,2048]{2,1,0:T(8,128)(2,1)S(1)}, u32[]{:S(2)}, u32[]{:S(2)}) %collective-permute-start.1) | collective-permute-done | bytes 524320 | tf_op jit(solution)/shard_map/ppermute | solution.py:21
  41.3 4.4 collective-permute-start.2
  45.7 9.4 %collective-permute-done.2 = bf16[2,64,2048]{2,1,0:T(8,128)(2,1)S(1)} collective-permute-done((bf16[2,64,2048]{2,1,0:T(8,128)(2,1)S(1)}, bf16[2,64,2048]{2,1,0:T(8,128)(2,1)S(1)}, u32[]{:S(2)}, u32[]{:S(2)}) %collective-permute-start.2) | collective-permute-done | bytes 524320 | tf_op jit(solution)/shard_map/ppermute | solution.py:21
  55.1 5.0 collective-permute-start.3
  62.3 6.3 %collective-permute-done.3 = bf16[2,64,2048]{2,1,0:T(8,128)(2,1)S(1)} collective-permute-done((bf16[2,64,2048]{2,1,0:T(8,128)(2,1)S(1)}, bf16[2,64,2048]{2,1,0:T(8,128)(2,1)S(1)}, u32[]{:S(2)}, u32[]{:S(2)}) %collective-permute-start.3) | collective-permute-done | bytes 524320 | tf_op jit(solution)/shard_map/ppermute | solution.py:21
  68.6 5.3 collective-permute-start.4
  74.1 3.1 gather_fusion
  77.4 4.0 collective-permute-done.4
  81.4 6.1 %collective-permute-start.5 = (bf16[2,64,2048]{2,1,0:T(8,128)(2,1)S(1)}, bf16[2,64,2048]{2,1,0:T(8,128)(2,1)}, u32[]{:S(2)}, u32[]{:S(2)}) collective-permute-start(bf16[2,64,2048]{2,1,0:T(8,128)(2,1)S(1)} %collective-permute-done.4), channel_id=1, source_target_pairs={{0,4},{4,8},{8,12},{12,16},{16,20},{20,24},{24,28},{1,5},{5,9},{9,... | collective-permute-start | bytes 1572872 | tf_op jit(solution)/shard_map/ppermute | solution.py:21
  87.7 5.6 %collective-permute-done.5 = bf16[2,64,2048]{2,1,0:T(8,128)(2,1)} collective-permute-done((bf16[2,64,2048]{2,1,0:T(8,128)(2,1)S(1)}, bf16[2,64,2048]{2,1,0:T(8,128)(2,1)}, u32[]{:S(2)}, u32[]{:S(2)}) %collective-permute-start.5) | collective-permute-done | bytes 524320 | tf_op jit(solution)/shard_map/ppermute | solution.py:21
  93.3 6.2 %collective-permute-start.6 = (bf16[2,64,2048]{2,1,0:T(8,128)(2,1)}, bf16[2,64,2048]{2,1,0:T(8,128)(2,1)}, u32[]{:S(2)}, u32[]{:S(2)}) collective-permute-start(bf16[2,64,2048]{2,1,0:T(8,128)(2,1)} %collective-permute-done.5), channel_id=1, source_target_pairs={{0,4},{4,8},{8,12},{12,16},{16,20},{20,24},{24,28},{1,5},{5,9},{9,... | collective-permute-start | bytes 1572872 | tf_op jit(solution)/shard_map/ppermute | solution.py:21
  100.6 5.2 collective-permute-done.6
  115.7 89.4 %while.57 = (s32[]{:T(128)}, f32[32,256]{1,0:T(8,128)S(1)}, f32[32,256]{1,0:T(8,128)S(1)}, f32[32,256]{1,0:T(8,128)S(1)}, pred[2,256,512]{1,2,0:T(8,128)(4,1)S(1...) while((s32[]{:T(128)}, f32[32,256]{1,0:T(8,128)S(1)}, ...), condition=%wide.region_4.5_spmd, body=%wide.region_0.4_spmd.sunk | while | flops 136837648 | bytes 13261259 | solution.py:153
  205.1 5.4 all-gather.2
  210.5 5.4 all-gather
  215.9 5.4 all-gather.1
  229.2 123.6 %while.59 = (s32[]{:T(128)}, f32[256,4096]{1,0:T(8,128)}, f32[512,2048]{1,0:T(8,128)}, f32[512,2048]{1,0:T(8,128)}, bf16[2,512,2048]{2,1,0:T(8,128)(2,1)}, /*ind...) while((s32[]{:T(128)}, f32[256,4096]{1,0:T(8,128)}, ...), condition=%wide.region_8.9_spmd, body=%wide.region_7.8_spmd.sunk | while | flops 338165792 | bytes 16796144 | solution.py:197
  363.9 22.0 %collective-permute-done.7 = f32[2,64,2048]{2,1,0:T(8,128)S(1)} collective-permute-done((f32[2,64,2048]{2,1,0:T(8,128)S(1)}, f32[2,64,2048]{2,1,0:T(8,128)S(1)}, u32[]{:S(2)}, u32[]{:S(2)}) %collective-permute-start.7) | collective-permute-done | bytes 1048608 | tf_op jit(solution)/shard_map/ppermute | solution.py:21
  387.2 23.1 %collective-permute-done.8 = f32[2,64,2048]{2,1,0:T(8,128)S(1)} collective-permute-done((f32[2,64,2048]{2,1,0:T(8,128)S(1)}, f32[2,64,2048]{2,1,0:T(8,128)S(1)}, u32[]{:S(2)}, u32[]{:S(2)}) %collective-permute-start.8) | collective-permute-done | bytes 1048608 | tf_op jit(solution)/shard_map/ppermute | solution.py:21
  413.5 132.6 %collective-permute-done.10 = f32[2,64,2048]{2,1,0:T(8,128)S(1)} collective-permute-done((f32[2,64,2048]{2,1,0:T(8,128)S(1)}, f32[2,64,2048]{2,1,0:T(8,128)S(1)}, u32[]{:S(2)}, u32[]{:S(2)}) %collective-permute-start.10) | collective-permute-done | bytes 1048608 | tf_op jit(solution)/shard_map/ppermute | solution.py:21
  546.1 3.4 collective-permute-done.11
  (427 shorter events, 252.9 us)
Async XLA Ops:
  7.2 66.8 %copy-start = (s32[2,16,14]{1,0,2:T(2,128)S(1)}, s32[2,16,14]{1,0,2:T(2,128)}, u32[]{:S(2)}) copy-start(s32[2,16,14]{1,0,2:T(2,128)} %param.17) | copy-start | bytes 5380
  7.2 66.8 %copy-start.2 = (s32[2048]{0:T(1024)S(1)}, s32[2048]{0:T(1024)}, u32[]{:S(2)}) copy-start(s32[2048]{0:T(1024)} %param.16) | copy-start | bytes 24580
  7.2 108.5 %all-gather.6.cloned.1.call-start = ((), (), s32[]{:S(2)}) async-start(), calls=%async_computation.1 | async-start | bytes 2621440 | tf_op jit(solution)/shard_map/all_gather | solution.py:99
  9.3 106.4 %all-gather.8.cloned.1.call-start = ((), (), s32[]{:S(2)}) async-start(), calls=%async_computation.2 | async-start | bytes 2621440 | tf_op jit(solution)/shard_map/all_gather | solution.py:100
  10.4 16.0 %collective-permute-start = (bf16[2,64,2048]{2,1,0:T(8,128)(2,1)S(1)}, bf16[2,64,2048]{2,1,0:T(8,128)(2,1)S(1)}, u32[]{:S(2)}, u32[]{:S(2)}) collective-permute-start(bf16[2,64,2048]{2,1,0:T(8,128)(2,1)S(1)} %pad_maximum_fusion.7), channel_id=1, source_target_pairs={{0,4},{4,8},{8,12},{12,16},{16,20},{20,24},{24,28},{1,5},{5,9},{9,... | collective-permute-start | bytes 1572872 | tf_op jit(solution)/shard_map/ppermute | solution.py:21
  26.5 14.8 %collective-permute-start.1 = (bf16[2,64,2048]{2,1,0:T(8,128)(2,1)S(1)}, bf16[2,64,2048]{2,1,0:T(8,128)(2,1)S(1)}, u32[]{:S(2)}, u32[]{:S(2)}) collective-permute-start(bf16[2,64,2048]{2,1,0:T(8,128)(2,1)S(1)} %collective-permute-done), channel_id=1, source_target_pairs={{0,4},{4,8},{8,12},{12,16},{16,20},{20,24},{24,28},{1,5},{5,9},{9,... | collective-permute-start | bytes 1572872 | tf_op jit(solution)/shard_map/ppermute | solution.py:21
  41.3 13.9 %collective-permute-start.2 = (bf16[2,64,2048]{2,1,0:T(8,128)(2,1)S(1)}, bf16[2,64,2048]{2,1,0:T(8,128)(2,1)S(1)}, u32[]{:S(2)}, u32[]{:S(2)}) collective-permute-start(bf16[2,64,2048]{2,1,0:T(8,128)(2,1)S(1)} %collective-permute-done.1), channel_id=1, source_target_pairs={{0,4},{4,8},{8,12},{12,16},{16,20},{20,24},{24,28},{1,5},{5,9},{9,... | collective-permute-start | bytes 1572872 | tf_op jit(solution)/shard_map/ppermute | solution.py:21
  55.1 13.5 %collective-permute-start.3 = (bf16[2,64,2048]{2,1,0:T(8,128)(2,1)S(1)}, bf16[2,64,2048]{2,1,0:T(8,128)(2,1)S(1)}, u32[]{:S(2)}, u32[]{:S(2)}) collective-permute-start(bf16[2,64,2048]{2,1,0:T(8,128)(2,1)S(1)} %collective-permute-done.2), channel_id=1, source_target_pairs={{0,4},{4,8},{8,12},{12,16},{16,20},{20,24},{24,28},{1,5},{5,9},{9,... | collective-permute-start | bytes 1572872 | tf_op jit(solution)/shard_map/ppermute | solution.py:21
  62.2 489.1 %reduce-scatter.2.cloned.1.call-start = ((), (), s32[]{:S(2)}) async-start(), calls=%async_computation.3 | async-start | bytes 5242880 | tf_op jit(solution)/shard_map/reduce_scatter | solution.py:200
  68.6 12.8 %collective-permute-start.4 = (bf16[2,64,2048]{2,1,0:T(8,128)(2,1)S(1)}, bf16[2,64,2048]{2,1,0:T(8,128)(2,1)S(1)}, u32[]{:S(2)}, u32[]{:S(2)}) collective-permute-start(bf16[2,64,2048]{2,1,0:T(8,128)(2,1)S(1)} %collective-permute-done.3), channel_id=1, source_target_pairs={{0,4},{4,8},{8,12},{12,16},{16,20},{20,24},{24,28},{1,5},{5,9},{9,... | collective-permute-start | bytes 1572872 | tf_op jit(solution)/shard_map/ppermute | solution.py:21
  81.4 18.3 %copy-start.6 = (bf16[2,64,2048]{2,1,0:T(8,128)(2,1)}, bf16[2,64,2048]{2,1,0:T(8,128)(2,1)S(1)}, u32[]{:S(2)}) copy-start(bf16[2,64,2048]{2,1,0:T(8,128)(2,1)S(1)} %collective-permute-done.4) | copy-start | bytes 1572868
  81.4 12.0 %collective-permute-start.5 = (bf16[2,64,2048]{2,1,0:T(8,128)(2,1)S(1)}, bf16[2,64,2048]{2,1,0:T(8,128)(2,1)}, u32[]{:S(2)}, u32[]{:S(2)}) collective-permute-start(bf16[2,64,2048]{2,1,0:T(8,128)(2,1)S(1)} %collective-permute-done.4), channel_id=1, source_target_pairs={{0,4},{4,8},{8,12},{12,16},{16,20},{20,24},{24,28},{1,5},{5,9},{9,... | collective-permute-start | bytes 1572872 | tf_op jit(solution)/shard_map/ppermute | solution.py:21
  93.3 12.4 %collective-permute-start.6 = (bf16[2,64,2048]{2,1,0:T(8,128)(2,1)}, bf16[2,64,2048]{2,1,0:T(8,128)(2,1)}, u32[]{:S(2)}, u32[]{:S(2)}) collective-permute-start(bf16[2,64,2048]{2,1,0:T(8,128)(2,1)} %collective-permute-done.5), channel_id=1, source_target_pairs={{0,4},{4,8},{8,12},{12,16},{16,20},{20,24},{24,28},{1,5},{5,9},{9,... | collective-permute-start | bytes 1572872 | tf_op jit(solution)/shard_map/ppermute | solution.py:21
  99.9 14.9 %copy-start.4 = (bf16[64,2048]{1,0:T(8,128)(2,1)S(1)}, bf16[64,2048]{1,0:T(8,128)(2,1)}, u32[]{:S(2)}) copy-start(bf16[64,2048]{1,0:T(8,128)(2,1)} %param.15) | copy-start | bytes 786436
  99.9 14.9 %copy-start.5 = (bf16[64,2048]{1,0:T(8,128)(2,1)S(1)}, bf16[64,2048]{1,0:T(8,128)(2,1)}, u32[]{:S(2)}) copy-start(bf16[64,2048]{1,0:T(8,128)(2,1)} %param.14) | copy-start | bytes 786436
  352.8 3.4 copy-start.3
  356.8 29.1 %collective-permute-start.7 = (f32[2,64,2048]{2,1,0:T(8,128)S(1)}, f32[2,64,2048]{2,1,0:T(8,128)S(1)}, u32[]{:S(2)}, u32[]{:S(2)}) collective-permute-start(f32[2,64,2048]{2,1,0:T(8,128)S(1)} %pad_maximum_fusion), channel_id=1, source_target_pairs={{4,0},{8,4},{12,8},{16,12},{20,16},{24,20},{28,24},{5,1},{9,5},{13... | collective-permute-start | bytes 3145736 | tf_op jit(solution)/shard_map/ppermute | solution.py:21
  358.2 52.0 %collective-permute-start.8 = (f32[2,64,2048]{2,1,0:T(8,128)S(1)}, f32[2,64,2048]{2,1,0:T(8,128)S(1)}, u32[]{:S(2)}, u32[]{:S(2)}) collective-permute-start(f32[2,64,2048]{2,1,0:T(8,128)S(1)} %pad_maximum_fusion.1), channel_id=1, source_target_pairs={{8,0},{12,4},{16,8},{20,12},{24,16},{28,20},{9,1},{13,5},{17,9},{2... | collective-permute-start | bytes 3145736 | tf_op jit(solution)/shard_map/ppermute | solution.py:21
  359.6 53.8 %collective-permute-start.9 = (f32[2,64,2048]{2,1,0:T(8,128)S(1)}, f32[2,64,2048]{2,1,0:T(8,128)S(1)}, u32[]{:S(2)}, u32[]{:S(2)}) collective-permute-start(f32[2,64,2048]{2,1,0:T(8,128)S(1)} %pad_maximum_fusion.2), channel_id=1, source_target_pairs={{12,0},{16,4},{20,8},{24,12},{28,16},{13,1},{17,5},{21,9},{25,13},... | collective-permute-start | bytes 3145736 | tf_op jit(solution)/shard_map/ppermute | solution.py:21
  361.0 185.1 %collective-permute-start.10 = (f32[2,64,2048]{2,1,0:T(8,128)S(1)}, f32[2,64,2048]{2,1,0:T(8,128)S(1)}, u32[]{:S(2)}, u32[]{:S(2)}) collective-permute-start(f32[2,64,2048]{2,1,0:T(8,128)S(1)} %pad_maximum_fusion.3), channel_id=1, source_target_pairs={{16,0},{20,4},{24,8},{28,12},{17,1},{21,5},{25,9},{29,13},{18,2},{... | collective-permute-start | bytes 3145736 | tf_op jit(solution)/shard_map/ppermute | solution.py:21
  362.4 187.0 %collective-permute-start.11 = (f32[2,64,2048]{2,1,0:T(8,128)S(1)}, f32[2,64,2048]{2,1,0:T(8,128)S(1)}, u32[]{:S(2)}, u32[]{:S(2)}) collective-permute-start(f32[2,64,2048]{2,1,0:T(8,128)S(1)} %pad_maximum_fusion.4), channel_id=1, source_target_pairs={{20,0},{24,4},{28,8},{21,1},{25,5},{29,9},{22,2},{26,6},{30,10},{2... | collective-permute-start | bytes 3145736 | tf_op jit(solution)/shard_map/ppermute | solution.py:21
  385.9 163.6 %collective-permute-start.12 = (f32[2,64,2048]{2,1,0:T(8,128)S(1)}, f32[2,64,2048]{2,1,0:T(8,128)S(1)}, u32[]{:S(2)}, u32[]{:S(2)}) collective-permute-start(f32[2,64,2048]{2,1,0:T(8,128)S(1)} %pad_maximum_fusion.5), channel_id=1, source_target_pairs={{24,0},{28,4},{25,1},{29,5},{26,2},{30,6},{27,3},{31,7}} | collective-permute-start | bytes 3145736 | tf_op jit(solution)/shard_map/ppermute | solution.py:21
  410.3 139.2 %collective-permute-start.13 = (f32[2,64,2048]{2,1,0:T(8,128)S(1)}, f32[2,64,2048]{2,1,0:T(8,128)S(1)}, u32[]{:S(2)}, u32[]{:S(2)}) collective-permute-start(f32[2,64,2048]{2,1,0:T(8,128)S(1)} %pad_maximum_fusion.6), channel_id=1, source_target_pairs={{28,0},{29,1},{30,2},{31,3}} | collective-permute-start | bytes 3145736 | tf_op jit(solution)/shard_map/ppermute | solution.py:21
  549.5 1.9 copy-start.1
Sparse Core Ops, SparseCore 0:
  10.2 25.2 all-gather.5
  62.3 24.6 all-gather.7
  352.9 48.6 reduce-scatter.1
where the time goes:
time: 560 us; the launch traced here: 558 us
  waiting for transfers between devices  235 us (42%)
  local copies, waits for them, and re-layouts  177 us (32%)
  matrix products  59.4 us (11%)
  starting transfers between devices  45.5 us (8%)
  blocking collectives  16.2 us (3%)
  between operations  14.1 us (3%)
  other arithmetic  7.8 us (1%)
    ppermute x14, waiting for transfers between devices, shifted(): return lax.ppermute(x, axis, pairs)  235 us
    slice x32, local copies, waits for them, and re-layouts, scores_for(): window[1]  87.2 us
    ppermute x14, starting transfers between devices, shifted(): return lax.ppermute(x, axis, pairs)  45.4 us
    dynamic_slice x32, local copies, waits for them, and re-layouts, scores_for(): lax.dynamic_slice_in_dim(full_grad, kv_head * head_cols, head_cols, 1)  30.6 us
    dot_general x16, matrix products, closing_sweep(): jnp.einsum('qrk,rqd->kd', probability_floor, grad_cols, preferred_element...  16.5 us
    dot_general x16, matrix products, closing_sweep(): jnp.einsum('qrk,rqd->kd', blended_rows, query_cols, preferred_element_typ...  16.5 us
    all_gather x3, blocking collectives, combined_all(): everything = jax.tree.map(lambda part: lax.all_gather(part, axis), x)  16.2 us
    dynamic_slice x16, local copies, waits for them, and re-layouts, scores_for(): lax.dynamic_slice_in_dim(full_q, kv_head * head_cols, head_cols, 1)  14.7 us
  transfers between devices with their start and end apart: 17, of which 12 were waited for; matrix products, arithmetic and copies ran while one was open for 4% of the time, Pallas kernels for 0%

commit v1 on v0

v1 whole, which is shorter than its diff:
```python
import functools

import jax
import jax.numpy as jnp
from jax import lax
from jax.experimental import pallas as pl
from jax.experimental.pallas import tpu as pltpu
from jax.sharding import PartitionSpec as P

QUERY_HEADS = 32
KEY_VALUE_HEADS = 16
HEAD_SIZE = 128
HEAD_GROUPS = 2
BLOCK_POSITIONS = 128
BACK = 14

SCORE_SCALE = 1.0 / 12.0
LOG2E = 1.4426950408889634
NEG_LARGE = -1e30
HIT = 1 << 20
NO_KEY = -(1 << 24)
TILE = 256
MESH = pl.DeviceIdType.MESH
VMEM_LIMIT = 48 * 1024 * 1024


class Place:
    def __init__(self, spans, ka_count):
        self.spans = spans
        self.ka_count = ka_count
        pb = lax.axis_index("pb")
        self.ka = lax.axis_index("ka")
        self.group = pb // spans
        self.span = pb % spans
        self.pair = self.ka // 2
        self.core = self.ka % 2
        self.head = self.pair * spans + self.span
        self.held = KEY_VALUE_HEADS // ka_count

    def at(self, span, ka):
        return {"pb": self.group * self.spans + span, "ka": ka}

    def greet(self):
        barrier = pltpu.get_barrier_semaphore()
        for t in range(1, self.spans * self.ka_count):
            pl.semaphore_signal(
                barrier,
                inc=1,
                device_id=self.at(
                    (self.span + t // self.ka_count) % self.spans,
                    (self.ka + t % self.ka_count) % self.ka_count,
                ),
                device_id_type=MESH,
            )
        pl.semaphore_wait(barrier, self.spans * self.ka_count - 1)


def wait_for(ref, sem):
    pltpu.make_async_copy(ref, ref, sem).wait()


def lanes(index):
    return pl.ds(pl.multiple_of(index * HEAD_SIZE, HEAD_SIZE), HEAD_SIZE)


def rows_at(begin, count):
    return pl.ds(pl.multiple_of(begin, count), count)


def gather_kernel(
    spans, ka_count, q, do, k, v, qh, doh, kh, vh, kv_send, kv_recv, q_send, q_recv, x_send, x_recv
):
    me = Place(spans, ka_count)
    tok = q.shape[0]
    piece = k.shape[0]
    me.greet()
    kv_rows = rows_at(me.span * tok + me.ka * piece, piece)
    for t in range(spans * ka_count // 2):
        span = (me.span + t % spans) % spans
        pair = (me.pair + t // spans) % (ka_count // 2)
        cols = lanes(pair * spans + span)
        for core, (src, dst) in enumerate(((k, kh), (v, vh))):

            def remote(src=src, dst=dst, core=core, span=span, pair=pair, cols=cols):
                pltpu.make_async_remote_copy(
                    src_ref=src.at[:, cols],
                    dst_ref=dst.at[kv_rows, :],
                    send_sem=kv_send,
                    recv_sem=kv_recv,
                    device_id=me.at(span, 2 * pair + core),
                    device_id_type=MESH,
                ).start()

            if t == 0:
                pl.when(me.core != core)(remote)

                @pl.when(me.core == core)
                def _(src=src, dst=dst, cols=cols):
                    pltpu.make_async_copy(src.at[:, cols], dst.at[kv_rows, :], kv_recv).start()
            else:
                remote()
    q_rows = rows_at(me.span * tok, tok)
    for j in range(me.held):
        near = (me.span + j) % me.held
        span = me.held * me.core + near
        for core in range(2):
            cols = lanes(2 * near + core)
            mine = (span == me.span) & (me.core == core)
            for which, (src, dst) in enumerate(((q, qh), (do, doh))):

                @pl.when(mine)
                def _(src=src, dst=dst, cols=cols, which=which):
                    pltpu.make_async_copy(
                        src.at[:, cols], dst.at[q_rows, :], q_recv.at[which]
                    ).start()

                @pl.when(jnp.logical_not(mine))
                def _(src=src, dst=dst, cols=cols, core=core, span=span, which=which):
                    pltpu.make_async_remote_copy(
                        src_ref=src.at[:, cols],
                        dst_ref=dst.at[q_rows, :],
                        send_sem=q_send.at[which],
                        recv_sem=q_recv.at[which],
                        device_id=me.at(span, 2 * me.pair + core),
                        device_id_type=MESH,
                    ).start()

    def exchange(ref):
        return pltpu.make_async_remote_copy(
            src_ref=ref,
            dst_ref=ref,
            send_sem=x_send,
            recv_sem=x_recv,
            device_id=me.at(me.span, 2 * me.pair + 1 - me.core),
            device_id_type=MESH,
        )

    for core, ref in enumerate((kh, vh)):

        @pl.when(me.core == core)
        def _(ref=ref):
            wait_for(ref, kv_recv)
            exchange(ref).start()

    wait_for(kh, x_recv)
    wait_for(kh, x_send)
    wait_for(kh.at[: (spans * ka_count - 1) * piece], kv_send)
    wait_for(qh, q_recv.at[0])
    wait_for(doh, q_recv.at[1])
    sent = 2 * me.held * tok
    has_own = me.span // me.held == me.core
    for which, ref in enumerate((qh, doh)):
        sem = q_send.at[which]
        pl.when(has_own)(lambda ref=ref, sem=sem: wait_for(ref.at[: sent - tok], sem))
        pl.when(jnp.logical_not(has_own))(lambda ref=ref, sem=sem: wait_for(ref.at[:sent], sem))


def attention_kernel(
    spans, ka_count, halo, listed, turn_row, turn_col, q, do, k, v, dq, dk, dv, kt, s_buf, g_buf
):
    me = Place(spans, ka_count)
    rows = q.shape[0]
    keys = k.shape[0]
    blocks = listed.shape[0] // (HEAD_GROUPS * BACK)
    head_group = me.head // (KEY_VALUE_HEADS // HEAD_GROUPS)
    list_base = (head_group * blocks + me.group * (rows // BLOCK_POSITIONS)) * BACK
    dk[...] = jnp.zeros_like(dk)
    dv[...] = jnp.zeros_like(dv)
    for n in range(keys // TILE):
        kt[:, n * TILE : (n + 1) * TILE] = k[n * TILE : (n + 1) * TILE, :].T
    left = lax.broadcasted_iota(jnp.int32, (1, TILE), 1) < BLOCK_POSITIONS
    causal = lax.broadcasted_iota(jnp.int32, (TILE, TILE), 0) <= lax.broadcasted_iota(
        jnp.int32, (TILE, TILE), 1
    )

    def hit(block, key_block):
        offset = block - key_block - 1
        if 0 <= offset < BACK:
            return listed[list_base + block * BACK + offset]
        return jnp.int32(0)

    for i in reversed(range(rows // TILE)):
        q_i = q[i * TILE : (i + 1) * TILE, :]
        do_i = do[i * TILE : (i + 1) * TILE, :]
        turn_i = turn_row[:, i * TILE : (i + 1) * TILE]
        last = halo // TILE + i
        first = max(0, last - BACK * BLOCK_POSITIONS // TILE)
        peak = jnp.full((8, TILE), NEG_LARGE, jnp.float32)
        for n in range(first, last + 1):
            at = slice(n * TILE, (n + 1) * TILE)
            s = lax.dot_general(
                k[at, :], q_i, (((1,), (1,)), ((), ())), preferred_element_type=jnp.float32
            ) * (SCORE_SCALE * LOG2E)
            parts = []
            for half in range(TILE // BLOCK_POSITIONS):
                key_block = 2 * n + half - halo // BLOCK_POSITIONS
                seen = jnp.where(left, hit(2 * i, key_block), hit(2 * i + 1, key_block))
                bar = turn_i - seen * HIT
                begin = n * TILE + half * BLOCK_POSITIONS
                turns = turn_col[begin : begin + BLOCK_POSITIONS, :]
                parts.append(jnp.concatenate([turns, turns], axis=1) >= bar)
            allowed = jnp.concatenate(parts, axis=0)
            if n == last:
                allowed = allowed & causal
            s = jnp.where(allowed, s, NEG_LARGE)
            s_buf[at, :] = s
            peak = jnp.maximum(peak, jnp.max(s.reshape(TILE // 8, 8, TILE), axis=0))
        peak = jnp.max(peak, axis=0, keepdims=True)
        total = jnp.zeros((8, TILE), jnp.float32)
        inner = jnp.zeros((8, TILE), jnp.float32)
        for n in range(first, last + 1):
            at = slice(n * TILE, (n + 1) * TILE)
            g = lax.dot_general(
                v[at, :], do_i, (((1,), (1,)), ((), ())), preferred_element_type=jnp.float32
            )
            p = jnp.exp2(s_buf[at, :] - peak)
            s_buf[at, :] = p
            g_buf[at, :] = g
            total = total + jnp.sum(p.reshape(TILE // 8, 8, TILE), axis=0)
            inner = inner + jnp.sum((p * g).reshape(TILE // 8, 8, TILE), axis=0)
        inverse = 1.0 / jnp.sum(total, axis=0, keepdims=True)
        delta = jnp.sum(inner, axis=0, keepdims=True) * inverse
        scaled = inverse * SCORE_SCALE
        dq_t = jnp.zeros((HEAD_SIZE, TILE), jnp.float32)
        for n in range(first, last + 1):
            at = slice(n * TILE, (n + 1) * TILE)
            p = s_buf[at, :]
            mixed = ((p * scaled) * (g_buf[at, :] - delta)).astype(jnp.bfloat16)
            low = (p * inverse).astype(jnp.bfloat16)
            dv[at, :] += jnp.dot(low, do_i, preferred_element_type=jnp.float32)
            dk[at, :] += jnp.dot(mixed, q_i, preferred_element_type=jnp.float32)
            dq_t = dq_t + jnp.dot(kt[:, at], mixed, preferred_element_type=jnp.float32)
        dq[i * TILE : (i + 1) * TILE, :] = dq_t.T.astype(jnp.bfloat16)


def scatter_kernel(
    spans, ka_count, dqh, dkh, dvh, dq, dk, dv, got, low, x_send, x_recv, q_send, q_recv, kv_send, kv_recv
):
    me = Place(spans, ka_count)
    tok = dq.shape[0]
    piece = dk.shape[0]
    me.greet()

    def exchange(ref):
        return pltpu.make_async_remote_copy(
            src_ref=ref,
            dst_ref=got,
            send_sem=x_send,
            recv_sem=x_recv,
            device_id=me.at(me.span, 2 * me.pair + 1 - me.core),
            device_id_type=MESH,
        )

    pl.when(me.core == 0)(lambda: exchange(dvh).start())
    pl.when(me.core == 1)(lambda: exchange(dkh).start())
    owner = 2 * me.pair + me.span // me.held
    cols = lanes(2 * (me.span % me.held) + me.core)
    for t in range(spans):
        span = (me.span + t) % spans
        src = dqh.at[rows_at(span * tok, tok), :]

        def remote(src=src, span=span):
            pltpu.make_async_remote_copy(
                src_ref=src,
                dst_ref=dq.at[:, cols],
                send_sem=q_send,
                recv_sem=q_recv,
                device_id=me.at(span, owner),
                device_id_type=MESH,
            ).start()

        if t == 0:
            pl.when(owner != me.ka)(remote)

            @pl.when(owner == me.ka)
            def _(src=src):
                pltpu.make_async_copy(src, dq.at[:, cols], q_recv).start()
        else:
            remote()
    wait_for(got, x_recv)
    for core, (own, out) in enumerate(((dkh, dk), (dvh, dv))):

        @pl.when(me.core == core)
        def _(own=own, out=out):
            low[...] = (own[...] + got[...]).astype(jnp.bfloat16)
            head_cols = lanes(me.head)
            for t in range(spans * ka_count):
                span = (me.span + t // ka_count) % spans
                ka = (me.ka + t % ka_count) % ka_count
                src = low.at[rows_at(span * tok + ka * piece, piece), :]
                dst = out.at[:, head_cols]
                if t == 0:
                    pltpu.make_async_copy(src, dst, kv_recv.at[core]).start()
                else:
                    pltpu.make_async_remote_copy(
                        src_ref=src,
                        dst_ref=dst,
                        send_sem=kv_send,
                        recv_sem=kv_recv.at[core],
                        device_id=me.at(span, ka),
                        device_id_type=MESH,
                    ).start()

    wait_for(got, x_send)
    sent = spans * tok
    pl.when(owner == me.ka)(lambda: wait_for(dqh.at[: sent - tok], q_send))
    pl.when(owner != me.ka)(lambda: wait_for(dqh.at[:sent], q_send))
    wait_for(dq, q_recv)
    wait_for(low.at[: (spans * ka_count - 1) * piece], kv_send)
    wait_for(dk, kv_recv.at[0])
    wait_for(dv, kv_recv.at[1])


def per_device(queries, output_gradient, key_states, value_inputs, turn_ids, listed):
    ka_count = lax.axis_size("ka")
    pb_count = lax.axis_size("pb")
    spans = 2 * KEY_VALUE_HEADS // ka_count
    groups = pb_count // spans
    tok = queries.shape[0]
    piece = key_states.shape[0]
    rows = spans * tok
    halo = rows if groups > 1 else 0
    bf16, f32 = jnp.bfloat16, jnp.float32
    any_space = pl.BlockSpec(memory_space=pl.ANY)
    vmem = pl.BlockSpec(memory_space=pltpu.VMEM)
    dma = pltpu.SemaphoreType.DMA
    head_rows = jax.ShapeDtypeStruct((rows, HEAD_SIZE), bf16)

    q, do, k, v = pl.pallas_call(
        functools.partial(gather_kernel, spans, ka_count),
        out_shape=[head_rows] * 4,
        in_specs=[any_space] * 4,
        out_specs=[any_space] * 4,
        scratch_shapes=[dma, dma, dma((2,)), dma((2,)), dma, dma],
        compiler_params=pltpu.CompilerParams(collective_id=0, has_side_effects=True),
        name="gather_heads",
    )(queries, output_gradient, key_states, value_inputs)

    group = lax.axis_index("pb") // spans
    if groups > 1:
        turn_own = lax.dynamic_slice_in_dim(turn_ids, group * rows, rows, 0)
        turn_before = lax.dynamic_slice_in_dim(
            turn_ids, jnp.maximum(group - 1, 0) * rows, rows, 0
        )
        turn_before = jnp.where(group > 0, turn_before, NO_KEY)
        turn_keys = jnp.concatenate([turn_before, turn_own])
        forward = [(i, i + spans) for i in range(pb_count - spans)]
        k_before, v_before = lax.ppermute(jnp.stack([k, v]), "pb", forward)
        k = jnp.concatenate([k_before, k])
        v = jnp.concatenate([v_before, v])
    else:
        turn_own = turn_keys = turn_ids
    keys = halo + rows
    key_grad = jax.ShapeDtypeStruct((keys, HEAD_SIZE), f32)
    dq, dk, dv = pl.pallas_call(
        functools.partial(attention_kernel, spans, ka_count, halo),
        out_shape=[head_rows, key_grad, key_grad],
        in_specs=[pl.BlockSpec(memory_space=pltpu.SMEM)] + [vmem] * 6,
        out_specs=[vmem] * 3,
        scratch_shapes=[
            pltpu.VMEM((HEAD_SIZE, keys), bf16),
            pltpu.VMEM((keys, TILE), f32),
            pltpu.VMEM((keys, TILE), f32),
        ],
        compiler_params=pltpu.CompilerParams(vmem_limit_bytes=VMEM_LIMIT),
        name="attention_backward",
    )(
        listed.reshape(-1),
        turn_own[None, :],
        jnp.broadcast_to(turn_keys[:, None], (keys, HEAD_SIZE)),
        q,
        do,
        k,
        v,
    )
    if groups > 1:
        back = [(i + spans, i) for i in range(pb_count - spans)]
        dk_later, dv_later = lax.ppermute(jnp.stack([dk[:halo], dv[:halo]]), "pb", back)
        dk = dk[halo:] + dk_later
        dv = dv[halo:] + dv_later

    out = pl.pallas_call(
        functools.partial(scatter_kernel, spans, ka_count),
        out_shape=[
            jax.ShapeDtypeStruct(queries.shape, bf16),
            jax.ShapeDtypeStruct(key_states.shape, bf16),
            jax.ShapeDtypeStruct(key_states.shape, bf16),
        ],
        in_specs=[vmem] * 3,
        out_specs=[any_space] * 3,
        scratch_shapes=[
            pltpu.VMEM((rows, HEAD_SIZE), f32),
            pltpu.VMEM((rows, HEAD_SIZE), bf16),
            dma,
            dma,
            dma,
            dma,
            dma,
            dma((2,)),
        ],
        compiler_params=pltpu.CompilerParams(
            collective_id=1, has_side_effects=True, vmem_limit_bytes=VMEM_LIMIT
        ),
        name="scatter_gradients",
    )(dq, dk, dv)
    return tuple(part.astype(f32) for part in out)


def solution(mesh):
    in_specs = (
        P("pb", "ka"),
        P("pb", "ka"),
        P(("pb", "ka"), None),
        P(("pb", "ka"), None),
        P(),
        P(),
    )
    out_specs = (P("pb", "ka"), P(("pb", "ka"), None), P(("pb", "ka"), None))
    return jax.shard_map(
        per_device, mesh=mesh, in_specs=in_specs, out_specs=out_specs, check_vma=False
    )
```

time: 560 us -> 87.4 us (0.16)
  waiting for transfers between devices: 235 us -> 0 us
  local copies, waits for them, and re-layouts: 177 us -> 5.97 us
  Pallas kernels: 0 us -> 76.8 us
  matrix products: 59.4 us -> 0 us
  starting transfers between devices: 45.5 us -> 0 us
  blocking collectives: 16.2 us -> 0 us
  between operations: 14.1 us -> 0.67 us
    ppermute x14 -> x0, waiting for transfers between devices: 235 us -> none  [shifted(): return lax.ppermute(x, axis, pairs)]
    slice x35 -> x0, local copies, waits for them, and re-layouts: 87.3 us -> none  [the longest x32 87.2 us: scores_for(): window[1]]
    pallas_call x0 -> x3, Pallas kernels: none -> 76.8 us  [the longest x1 41.3 us: per_device(): pl.pallas_call(functools.partial(gather_kernel, spans, ka_count), out_sha...]
    dot_general x113 -> x0, matrix products: 59.4 us -> none  [the longest x16 16.5 us: closing_sweep(): jnp.einsum('qrk,rqd->kd', probability_floor, grad_cols, preferred_element...]
    dynamic_slice x82 -> x0, local copies, waits for them, and re-layouts: 45.7 us -> none  [the longest x32 30.6 us: scores_for(): lax.dynamic_slice_in_dim(full_grad, kv_head * head_cols, head_cols, 1)]
    ppermute x14 -> x0, starting transfers between devices: 45.4 us -> none  [shifted(): return lax.ppermute(x, axis, pairs)]
    all_gather x3 -> x0, blocking collectives: 16.2 us -> none  [combined_all(): everything = jax.tree.map(lambda part: lax.all_gather(part, axis), x)]
    dynamic_update_slice x64 -> x0, local copies, waits for them, and re-layouts: 14.6 us -> none  [the longest x32 14.2 us: closing_sweep(): lax.dynamic_update_slice_in_dim(query_gradient, grad_q_head, kv_head * he...]
  transfers between devices with their start and end apart: 17 -> 0, of which waited for: 12 -> 0; matrix products, arithmetic and copies ran while one was open for 4% -> 0% of each run, Pallas kernels for 0% -> 0%
where the time goes in v1:
time: 87.4 us; the launch traced here: 86.2 us
  Pallas kernels  76.8 us (88%)
  local copies, waits for them, and re-layouts  5.97 us (7%)
  other arithmetic  2.74 us (3%)
    pallas_call x1, Pallas kernels, per_device(): pl.pallas_call(functools.partial(gather_kernel, spans, ka_count), out_sha...  41.3 us
    pallas_call x1, Pallas kernels, per_device(): pl.pallas_call(functools.partial(scatter_kernel, spans, ka_count), out_sh...  25.5 us
    pallas_call x1, Pallas kernels, per_device(): pl.pallas_call(functools.partial(attention_kernel, spans, ka_count, halo)...  10 us
    unnamed x11, local copies, waits for them, and re-layouts  5.54 us
    convert_element_type x3, other arithmetic, per_device(): return tuple((part.astype(f32) for part in out))  2.74 us

profile of v1, /device:TPU:0, one launch (start us, length us, event | category | flops | bytes accessed | tf_op | source)
XLA Modules:
  0.0 86.2 jit_solution(17793254899699842577)
XLA Ops:
  0.6 0.8 copy.9
  1.4 0.0 copy-start.4
  1.4 0.1 reshape.10.listed
  1.5 0.6 copy-done.4
  2.1 0.3 broadcast_in_dim.10.turn_col
  2.5 41.3 %gather_heads.1 = (bf16[2048,128]{1,0:T(8,128)(2,1)}, bf16[2048,128]{1,0:T(8,128)(2,1)}, bf16[2048,128]{1,0:T(8,128)(2,1)}, bf16[2048,128]{1,0:T(8,128)(2,1)}) custom-call(bf16[256,1024]{1,0:T(8,128)(2,1)} %q.1, bf16[256,1024]{1,0:T(8,128)(2,1)} %do.1, bf16[64,2048]{1,0:T(8,128)(2,1)} %k.1, bf16[64,2048]{1,0:T(8,128)(2,1)} %v.1), custom_call_target="tpu_custom_call" | custom-call | tf_op jit(solution)/shard_map/gather_heads/pallas_call | solution.py:329
  43.7 0.0 copy-start
  43.7 1.0 %copy-done = bf16[2048,128]{1,0:T(8,128)(2,1)S(1)} copy-done((bf16[2048,128]{1,0:T(8,128)(2,1)S(1)}, bf16[2048,128]{1,0:T(8,128)(2,1)}, u32[]{:S(2)}) %copy-start) | copy-done | bytes 524312
  44.8 0.0 copy-start.1
  44.8 1.0 %copy-done.1 = bf16[2048,128]{1,0:T(8,128)(2,1)S(1)} copy-done((bf16[2048,128]{1,0:T(8,128)(2,1)S(1)}, bf16[2048,128]{1,0:T(8,128)(2,1)}, u32[]{:S(2)}) %copy-start.1) | copy-done | bytes 524312
  45.8 0.0 copy-start.2
  45.8 1.0 %copy-done.2 = bf16[2048,128]{1,0:T(8,128)(2,1)S(1)} copy-done((bf16[2048,128]{1,0:T(8,128)(2,1)S(1)}, bf16[2048,128]{1,0:T(8,128)(2,1)}, u32[]{:S(2)}) %copy-start.2) | copy-done | bytes 524312
  46.9 0.0 copy-start.3
  46.9 1.0 %copy-done.3 = bf16[2048,128]{1,0:T(8,128)(2,1)S(1)} copy-done((bf16[2048,128]{1,0:T(8,128)(2,1)S(1)}, bf16[2048,128]{1,0:T(8,128)(2,1)}, u32[]{:S(2)}) %copy-start.3) | copy-done | bytes 524312
  47.9 10.0 %attention_backward.1 = (bf16[2048,128]{1,0:T(8,128)(2,1)S(1)}, f32[2048,128]{1,0:T(8,128)S(1)}, f32[2048,128]{1,0:T(8,128)S(1)}) custom-call(s32[448]{0:T(512)S(1)} %reshape.10.listed, s32[1,2048]{1,0:T(1,128)S(1)} %bitcast.1, s32[2048,128]{1,0:T(8,128)S(1)} %broadcast_in_dim.10.turn_col, bf16[2048,128]{1,0:T(8,128)(2,1)S(1)} %copy-done, ...), custom_call_target="tpu_custom_call" | custom-call | tf_op jit(solution)/shard_map/attention_backward/pallas_call | solution.py:355
  57.9 25.5 %scatter_gradients.1 = (bf16[256,1024]{1,0:T(8,128)(2,1)S(1)}, bf16[64,2048]{1,0:T(8,128)(2,1)S(1)}, bf16[64,2048]{1,0:T(8,128)(2,1)S(1)}) custom-call(bf16[2048,128]{1,0:T(8,128)(2,1)S(1)} %get-tuple-element.17.dqh, f32[2048,128]{1,0:T(8,128)S(1)} %get-tuple-element.18.dkh, f32[2048,128]{1,0:T(8,128)S(1)} %get-tuple-element.19.dvh), custom_call_target="tpu_custom_call" | custom-call | tf_op jit(solution)/shard_map/scatter_gradients/pallas_call | solution.py:382
  83.4 1.1 %convert_element_type.9 = f32[256,1024]{1,0:T(8,128)} convert(bf16[256,1024]{1,0:T(8,128)(2,1)S(1)} %get-tuple-element.20) | non-fusion elementwise | flops 262144 | bytes 1572864 | tf_op jit(solution)/shard_map/convert_element_type | solution.py:406
  84.5 0.8 convert_element_type.10
  85.3 0.8 convert_element_type.11
Async XLA Ops:
  1.4 0.7 copy-start.4
  43.7 1.0 %copy-start = (bf16[2048,128]{1,0:T(8,128)(2,1)S(1)}, bf16[2048,128]{1,0:T(8,128)(2,1)}, u32[]{:S(2)}) copy-start(bf16[2048,128]{1,0:T(8,128)(2,1)} %get-tuple-element.13.q) | copy-start | bytes 1572868
  44.8 1.0 %copy-start.1 = (bf16[2048,128]{1,0:T(8,128)(2,1)S(1)}, bf16[2048,128]{1,0:T(8,128)(2,1)}, u32[]{:S(2)}) copy-start(bf16[2048,128]{1,0:T(8,128)(2,1)} %get-tuple-element.14.do) | copy-start | bytes 1572868
  45.8 1.0 %copy-start.2 = (bf16[2048,128]{1,0:T(8,128)(2,1)S(1)}, bf16[2048,128]{1,0:T(8,128)(2,1)}, u32[]{:S(2)}) copy-start(bf16[2048,128]{1,0:T(8,128)(2,1)} %get-tuple-element.15.k) | copy-start | bytes 1572868
  46.9 1.0 %copy-start.3 = (bf16[2048,128]{1,0:T(8,128)(2,1)S(1)}, bf16[2048,128]{1,0:T(8,128)(2,1)}, u32[]{:S(2)}) copy-start(bf16[2048,128]{1,0:T(8,128)(2,1)} %get-tuple-element.16.v) | copy-start | bytes 1572868

commit v2 on v1

--- a/solution.py
+++ b/solution.py
@@ -17,8 +17,8 @@
 SCORE_SCALE = 1.0 / 12.0
 LOG2E = 1.4426950408889634
 NEG_LARGE = -1e30
-HIT = 1 << 20
-NO_KEY = -(1 << 24)
+HIT = float(1 << 20)
+NO_KEY = -(1 << 22)
 TILE = 256
 MESH = pl.DeviceIdType.MESH
 VMEM_LIMIT = 48 * 1024 * 1024
@@ -67,18 +67,14 @@
     return pl.ds(pl.multiple_of(begin, count), count)
 
 
-def gather_kernel(
-    spans, ka_count, q, do, k, v, qh, doh, kh, vh, kv_send, kv_recv, q_send, q_recv, x_send, x_recv
-):
-    me = Place(spans, ka_count)
+def send_heads(me, q, do, k, v, qh, doh, kh, vh, kv_send, kv_recv, q_send, q_recv):
     tok = q.shape[0]
     piece = k.shape[0]
-    me.greet()
     kv_rows = rows_at(me.span * tok + me.ka * piece, piece)
-    for t in range(spans * ka_count // 2):
-        span = (me.span + t % spans) % spans
-        pair = (me.pair + t // spans) % (ka_count // 2)
-        cols = lanes(pair * spans + span)
+    for t in range(me.spans * me.ka_count // 2):
+        span = (me.span + t % me.spans) % me.spans
+        pair = (me.pair + t // me.spans) % (me.ka_count // 2)
+        cols = lanes(pair * me.spans + span)
         for core, (src, dst) in enumerate(((k, kh), (v, vh))):
 
             def remote(src=src, dst=dst, core=core, span=span, pair=pair, cols=cols):
@@ -107,46 +103,49 @@
             cols = lanes(2 * near + core)
             mine = (span == me.span) & (me.core == core)
             for which, (src, dst) in enumerate(((q, qh), (do, doh))):
+                sem = q_recv.at[which, me.span]
 
                 @pl.when(mine)
-                def _(src=src, dst=dst, cols=cols, which=which):
-                    pltpu.make_async_copy(
-                        src.at[:, cols], dst.at[q_rows, :], q_recv.at[which]
-                    ).start()
+                def _(src=src, dst=dst, cols=cols, sem=sem):
+                    pltpu.make_async_copy(src.at[:, cols], dst.at[q_rows, :], sem).start()
 
                 @pl.when(jnp.logical_not(mine))
-                def _(src=src, dst=dst, cols=cols, core=core, span=span, which=which):
+                def _(src=src, dst=dst, cols=cols, core=core, span=span, which=which, sem=sem):
                     pltpu.make_async_remote_copy(
                         src_ref=src.at[:, cols],
                         dst_ref=dst.at[q_rows, :],
                         send_sem=q_send.at[which],
-                        recv_sem=q_recv.at[which],
+                        recv_sem=sem,
                         device_id=me.at(span, 2 * me.pair + core),
                         device_id_type=MESH,
                     ).start()
 
-    def exchange(ref):
-        return pltpu.make_async_remote_copy(
-            src_ref=ref,
-            dst_ref=ref,
-            send_sem=x_send,
-            recv_sem=x_recv,
-            device_id=me.at(me.span, 2 * me.pair + 1 - me.core),
-            device_id_type=MESH,
-        )
-
+
+def to_other_core(me, src, dst, send_sem, recv_sem):
+    return pltpu.make_async_remote_copy(
+        src_ref=src,
+        dst_ref=dst,
+        send_sem=send_sem,
+        recv_sem=recv_sem,
+        device_id=me.at(me.span, 2 * me.pair + 1 - me.core),
+        device_id_type=MESH,
+    )
+
+
+def share_keys(me, kh, vh, kv_recv, x_send, x_recv):
     for core, ref in enumerate((kh, vh)):
 
         @pl.when(me.core == core)
         def _(ref=ref):
             wait_for(ref, kv_recv)
-            exchange(ref).start()
+            to_other_core(me, ref, ref, x_send, x_recv).start()
 
     wait_for(kh, x_recv)
+
+
+def finish_heads(me, qh, doh, kh, kv_send, q_send, x_send, tok, piece):
     wait_for(kh, x_send)
-    wait_for(kh.at[: (spans * ka_count - 1) * piece], kv_send)
-    wait_for(qh, q_recv.at[0])
-    wait_for(doh, q_recv.at[1])
+    wait_for(kh.at[: (me.spans * me.ka_count - 1) * piece], kv_send)
     sent = 2 * me.held * tok
     has_own = me.span // me.held == me.core
     for which, ref in enumerate((qh, doh)):
@@ -155,10 +154,147 @@
         pl.when(jnp.logical_not(has_own))(lambda ref=ref, sem=sem: wait_for(ref.at[:sent], sem))
 
 
-def attention_kernel(
-    spans, ka_count, halo, listed, turn_row, turn_col, q, do, k, v, dq, dk, dv, kt, s_buf, g_buf
+def gather_kernel(
+    spans, ka_count, q, do, k, v, qh, doh, kh, vh, kv_send, kv_recv, q_send, q_recv, x_send, x_recv
 ):
     me = Place(spans, ka_count)
+    tok = q.shape[0]
+    me.greet()
+    send_heads(me, q, do, k, v, qh, doh, kh, vh, kv_send, kv_recv, q_send, q_recv)
+    share_keys(me, kh, vh, kv_recv, x_send, x_recv)
+    for span in range(spans):
+        wait_for(qh.at[span * tok : (span + 1) * tok], q_recv.at[0, span])
+        wait_for(doh.at[span * tok : (span + 1) * tok], q_recv.at[1, span])
+    finish_heads(me, qh, doh, kh, kv_send, q_send, x_send, tok, k.shape[0])
+
+
+def fused_kernel(
+    spans, ka_count, listed, turn_row, q, do, k, v, dq, dk, dv,
+    qh, doh, kh, vh, turn_col, kt, s_buf, g_buf, dqh, dkh, dvh, got, low,
+    kv_send, kv_recv, q_send, q_recv, k_send, k_recv,
+    x_send, x_recv, dq_send, dq_recv, dkv_send, dkv_recv,
+):
+    me = Place(spans, ka_count)
+    tok = q.shape[0]
+    piece = k.shape[0]
+    me.greet()
+    send_heads(me, q, do, k, v, qh, doh, kh, vh, kv_send, kv_recv, q_send, q_recv)
+    for n in range(turn_col.shape[0] // HEAD_SIZE):
+        at = slice(n * HEAD_SIZE, (n + 1) * HEAD_SIZE)
+        turn_col[at, :] = jnp.broadcast_to(turn_row[:, at], (HEAD_SIZE, HEAD_SIZE)).T
+    share_keys(me, kh, vh, kv_recv, k_send, k_recv)
+    owner = 2 * me.pair + me.span // me.held
+    q_cols = lanes(2 * (me.span % me.held) + me.core)
+    head_cols = lanes(me.head)
+
+    def ready(i):
+        wait_for(qh.at[i * tok : (i + 1) * tok], q_recv.at[0, i])
+        wait_for(doh.at[i * tok : (i + 1) * tok], q_recv.at[1, i])
+
+    def send_queries(i):
+        src = dqh.at[i * tok : (i + 1) * tok, :]
+        mine = (me.span == i) & (owner == me.ka)
+
+        @pl.when(mine)
+        def _():
+            pltpu.make_async_copy(src, dq.at[:, q_cols], dq_recv).start()
+
+        @pl.when(jnp.logical_not(mine))
+        def _():
+            pltpu.make_async_remote_copy(
+                src_ref=src,
+                dst_ref=dq.at[:, q_cols],
+                send_sem=dq_send,
+                recv_sem=dq_recv,
+                device_id=me.at(i, owner),
+                device_id_type=MESH,
+            ).start()
+
+    def share_grads(j):
+        at = slice(j * tok, (j + 1) * tok)
+        for core, ref in enumerate((dvh, dkh)):
+
+            @pl.when(me.core == core)
+            def _(ref=ref):
+                to_other_core(me, ref.at[at], got.at[at], x_send, x_recv.at[j]).start()
+
+    def send_grads(j):
+        at = slice(j * tok, (j + 1) * tok)
+        wait_for(got.at[at], x_recv.at[j])
+        for core, (own, out) in enumerate(((dkh, dk), (dvh, dv))):
+
+            @pl.when(me.core == core)
+            def _(own=own, out=out, core=core):
+                low[at, :] = (own[at, :] + got[at, :]).astype(jnp.bfloat16)
+                for t in range(ka_count):
+                    ka = (me.ka + t) % ka_count
+                    src = low.at[rows_at(j * tok + ka * piece, piece), :]
+                    dst = out.at[:, head_cols]
+
+                    def remote(src=src, dst=dst, ka=ka):
+                        pltpu.make_async_remote_copy(
+                            src_ref=src,
+                            dst_ref=dst,
+                            send_sem=dkv_send,
+                            recv_sem=dkv_recv.at[core],
+                            device_id=me.at(j, ka),
+                            device_id_type=MESH,
+                        ).start()
+
+                    if t == 0:
+                        pl.when(me.span != j)(remote)
+
+                        @pl.when(me.span == j)
+                        def _(src=src, dst=dst):
+                            pltpu.make_async_copy(src, dst, dkv_recv.at[core]).start()
+                    else:
+                        remote()
+
+    half = spans // 2
+    order = [spans - 1, *range(half), *range(spans - 2, half - 1, -1)]
+    done = set()
+    shared = []
+
+    def after(i):
+        send_queries(i)
+        done.add(i)
+        for j in shared:
+            send_grads(j)
+        shared.clear()
+        for j in range(spans - 1, -1, -1):
+            if j not in started and all(n in done for n in range(j, spans)):
+                share_grads(j)
+                started.add(j)
+                shared.append(j)
+
+    started = set()
+    attend(
+        me, 0, order, ready, after,
+        listed, turn_row, turn_col, qh, doh, kh, vh, dqh, dkh, dvh, kt, s_buf, g_buf,
+    )
+    for j in shared:
+        send_grads(j)
+    finish_heads(me, qh, doh, kh, kv_send, q_send, k_send, tok, piece)
+    wait_for(got, x_send)
+    sent = spans * tok
+    pl.when(owner == me.ka)(lambda: wait_for(dqh.at[: sent - tok], dq_send))
+    pl.when(owner != me.ka)(lambda: wait_for(dqh.at[:sent], dq_send))
+    wait_for(low.at[: (spans * ka_count - 1) * piece], dkv_send)
+    wait_for(dq, dq_recv)
+    wait_for(dk, dkv_recv.at[0])
+    wait_for(dv, dkv_recv.at[1])
+
+
+def attention_kernel(spans, ka_count, halo, *refs):
+    order = list(range(refs[3].shape[0] // TILE))
+    nothing = lambda i: None
+    attend(Place(spans, ka_count), halo, order, nothing, nothing, *refs)
+
+
+def attend(
+    me, halo, order, ready, after,
+    listed, turn_row, turn_col, q, do, k, v, dq, dk, dv, kt, s_buf, g_buf,
+):
     rows = q.shape[0]
     keys = k.shape[0]
     blocks = listed.shape[0] // (HEAD_GROUPS * BACK)
@@ -179,7 +315,8 @@
             return listed[list_base + block * BACK + offset]
         return jnp.int32(0)
 
-    for i in reversed(range(rows // TILE)):
+    for i in order:
+        ready(i)
         q_i = q[i * TILE : (i + 1) * TILE, :]
         do_i = do[i * TILE : (i + 1) * TILE, :]
         turn_i = turn_row[:, i * TILE : (i + 1) * TILE]
@@ -195,7 +332,7 @@
             for half in range(TILE // BLOCK_POSITIONS):
                 key_block = 2 * n + half - halo // BLOCK_POSITIONS
                 seen = jnp.where(left, hit(2 * i, key_block), hit(2 * i + 1, key_block))
-                bar = turn_i - seen * HIT
+                bar = turn_i - seen.astype(jnp.float32) * HIT
                 begin = n * TILE + half * BLOCK_POSITIONS
                 turns = turn_col[begin : begin + BLOCK_POSITIONS, :]
                 parts.append(jnp.concatenate([turns, turns], axis=1) >= bar)
@@ -231,6 +368,7 @@
             dk[at, :] += jnp.dot(mixed, q_i, preferred_element_type=jnp.float32)
             dq_t = dq_t + jnp.dot(kt[:, at], mixed, preferred_element_type=jnp.float32)
         dq[i * TILE : (i + 1) * TILE, :] = dq_t.T.astype(jnp.bfloat16)
+        after(i)
 
 
 def scatter_kernel(
@@ -319,37 +457,83 @@
     tok = queries.shape[0]
     piece = key_states.shape[0]
     rows = spans * tok
-    halo = rows if groups > 1 else 0
+    halo = rows
     bf16, f32 = jnp.bfloat16, jnp.float32
     any_space = pl.BlockSpec(memory_space=pl.ANY)
     vmem = pl.BlockSpec(memory_space=pltpu.VMEM)
     dma = pltpu.SemaphoreType.DMA
     head_rows = jax.ShapeDtypeStruct((rows, HEAD_SIZE), bf16)
+    grads = [
+        jax.ShapeDtypeStruct(queries.shape, bf16),
+        jax.ShapeDtypeStruct(key_states.shape, bf16),
+        jax.ShapeDtypeStruct(key_states.shape, bf16),
+    ]
+    low_rows = pltpu.VMEM((rows, HEAD_SIZE), bf16)
+    full_rows = pltpu.VMEM((rows, HEAD_SIZE), f32)
+
+    if groups == 1:
+        out = pl.pallas_call(
+            functools.partial(fused_kernel, spans, ka_count),
+            out_shape=grads,
+            in_specs=[pl.BlockSpec(memory_space=pltpu.SMEM), vmem] + [any_space] * 4,
+            out_specs=[any_space] * 3,
+            scratch_shapes=[low_rows] * 4
+            + [
+                full_rows,
+                pltpu.VMEM((HEAD_SIZE, rows), bf16),
+                pltpu.VMEM((rows, TILE), f32),
+                pltpu.VMEM((rows, TILE), f32),
+                low_rows,
+                full_rows,
+                full_rows,
+                full_rows,
+                low_rows,
+                dma,
+                dma,
+                dma((2,)),
+                dma((2, spans)),
+                dma,
+                dma,
+                dma,
+                dma((spans,)),
+                dma,
+                dma,
+                dma,
+                dma((2,)),
+            ],
+            compiler_params=pltpu.CompilerParams(
+                collective_id=2, has_side_effects=True, vmem_limit_bytes=VMEM_LIMIT
+            ),
+            name="heads_backward",
+        )(
+            listed.reshape(-1),
+            turn_ids.astype(f32)[None, :],
+            queries,
+            output_gradient,
+            key_states,
+            value_inputs,
+        )
+        return tuple(part.astype(f32) for part in out)
 
     q, do, k, v = pl.pallas_call(
         functools.partial(gather_kernel, spans, ka_count),
         out_shape=[head_rows] * 4,
         in_specs=[any_space] * 4,
         out_specs=[any_space] * 4,
-        scratch_shapes=[dma, dma, dma((2,)), dma((2,)), dma, dma],
+        scratch_shapes=[dma, dma, dma((2,)), dma((2, spans)), dma, dma],
         compiler_params=pltpu.CompilerParams(collective_id=0, has_side_effects=True),
         name="gather_heads",
     )(queries, output_gradient, key_states, value_inputs)
 
     group = lax.axis_index("pb") // spans
-    if groups > 1:
-        turn_own = lax.dynamic_slice_in_dim(turn_ids, group * rows, rows, 0)
-        turn_before = lax.dynamic_slice_in_dim(
-            turn_ids, jnp.maximum(group - 1, 0) * rows, rows, 0
-        )
-        turn_before = jnp.where(group > 0, turn_before, NO_KEY)
-        turn_keys = jnp.concatenate([turn_before, turn_own])
-        forward = [(i, i + spans) for i in range(pb_count - spans)]
-        k_before, v_before = lax.ppermute(jnp.stack([k, v]), "pb", forward)
-        k = jnp.concatenate([k_before, k])
-        v = jnp.concatenate([v_before, v])
-    else:
-        turn_own = turn_keys = turn_ids
+    turn_own = lax.dynamic_slice_in_dim(turn_ids, group * rows, rows, 0)
+    turn_before = lax.dynamic_slice_in_dim(turn_ids, jnp.maximum(group - 1, 0) * rows, rows, 0)
+    turn_before = jnp.where(group > 0, turn_before, NO_KEY)
+    turn_keys = jnp.concatenate([turn_before, turn_own])
+    forward = [(i, i + spans) for i in range(pb_count - spans)]
+    k_before, v_before = lax.ppermute(jnp.stack([k, v]), "pb", forward)
+    k = jnp.concatenate([k_before, k])
+    v = jnp.concatenate([v_before, v])
     keys = halo + rows
     key_grad = jax.ShapeDtypeStruct((keys, HEAD_SIZE), f32)
     dq, dk, dv = pl.pallas_call(
@@ -366,26 +550,21 @@
         name="attention_backward",
     )(
         listed.reshape(-1),
-        turn_own[None, :],
-        jnp.broadcast_to(turn_keys[:, None], (keys, HEAD_SIZE)),
+        turn_own.astype(f32)[None, :],
+        jnp.broadcast_to(turn_keys.astype(f32)[:, None], (keys, HEAD_SIZE)),
         q,
         do,
         k,
         v,
     )
-    if groups > 1:
-        back = [(i + spans, i) for i in range(pb_count - spans)]
-        dk_later, dv_later = lax.ppermute(jnp.stack([dk[:halo], dv[:halo]]), "pb", back)
-        dk = dk[halo:] + dk_later
-        dv = dv[halo:] + dv_later
+    back = [(i + spans, i) for i in range(pb_count - spans)]
+    dk_later, dv_later = lax.ppermute(jnp.stack([dk[:halo], dv[:halo]]), "pb", back)
+    dk = dk[halo:] + dk_later
+    dv = dv[halo:] + dv_later
 
     out = pl.pallas_call(
         functools.partial(scatter_kernel, spans, ka_count),
-        out_shape=[
-            jax.ShapeDtypeStruct(queries.shape, bf16),
-            jax.ShapeDtypeStruct(key_states.shape, bf16),
-            jax.ShapeDtypeStruct(key_states.shape, bf16),
-        ],
+        out_shape=grads,
         in_specs=[vmem] * 3,
         out_specs=[any_space] * 3,
         scratch_shapes=[

time: 87.4 us -> 87.6 us (level); the launches traced: 86.2 us -> 87.3 us
  Pallas kernels: 76.8 us -> 79 us
  local copies, waits for them, and re-layouts: 5.97 us -> 4.17 us
    pallas_call x3 -> x1, Pallas kernels: 76.8 us -> 79 us  [per_device(): pl.pallas_call(functools.partial(fused_kernel, spans, ka_count), out_shap...]
    unnamed x11, local copies, waits for them, and re-layouts: 5.54 us -> 4.07 us
where the time goes in v2:
time: 87.6 us; the launch traced here: 87.3 us
  Pallas kernels  79 us (90%)
  local copies, waits for them, and re-layouts  4.17 us (5%)
  other arithmetic  3.44 us (4%)
    pallas_call x1, Pallas kernels, per_device(): pl.pallas_call(functools.partial(fused_kernel, spans, ka_count), out_shap...  79 us
    unnamed x11, local copies, waits for them, and re-layouts  4.07 us
    convert_element_type x3, other arithmetic, per_device(): return tuple((part.astype(f32) for part in out))  2.74 us

profile of v2, /device:TPU:0, one launch (start us, length us, event | category | flops | bytes accessed | tf_op | source)
XLA Modules:
  0.0 87.3 jit_solution(9477440535981242070)
XLA Ops:
  0.6 0.0 copy-start.4
  0.6 0.7 convert_element_type.12
  1.3 0.0 copy-done.4
  1.3 0.1 copy.9
  1.4 0.1 reshape.9.listed
  1.5 0.0 copy-start
  1.6 1.0 %copy-done = bf16[256,1024]{1,0:T(8,128)(2,1)S(1)} copy-done((bf16[256,1024]{1,0:T(8,128)(2,1)S(1)}, bf16[256,1024]{1,0:T(8,128)(2,1)}, u32[]{:S(2)}) %copy-start) | copy-done | bytes 524312
  2.6 0.0 copy-start.1
  2.6 1.0 %copy-done.1 = bf16[256,1024]{1,0:T(8,128)(2,1)S(1)} copy-done((bf16[256,1024]{1,0:T(8,128)(2,1)S(1)}, bf16[256,1024]{1,0:T(8,128)(2,1)}, u32[]{:S(2)}) %copy-start.1) | copy-done | bytes 524312
  3.6 0.0 copy-start.2
  3.6 0.9 %copy-done.2 = bf16[64,2048]{1,0:T(8,128)(2,1)S(1)} copy-done((bf16[64,2048]{1,0:T(8,128)(2,1)S(1)}, bf16[64,2048]{1,0:T(8,128)(2,1)}, u32[]{:S(2)}) %copy-start.2) | copy-done | bytes 262168
  4.6 0.0 copy-start.3
  4.6 0.9 %copy-done.3 = bf16[64,2048]{1,0:T(8,128)(2,1)S(1)} copy-done((bf16[64,2048]{1,0:T(8,128)(2,1)S(1)}, bf16[64,2048]{1,0:T(8,128)(2,1)}, u32[]{:S(2)}) %copy-start.3) | copy-done | bytes 262168
  5.5 79.0 %heads_backward.1 = (bf16[256,1024]{1,0:T(8,128)(2,1)S(1)}, bf16[64,2048]{1,0:T(8,128)(2,1)S(1)}, bf16[64,2048]{1,0:T(8,128)(2,1)S(1)}) custom-call(s32[448]{0:T(512)S(1)} %reshape.9.listed, f32[1,2048]{1,0:T(1,128)S(1)} %bitcast.1, bf16[256,1024]{1,0:T(8,128)(2,1)S(1)} %copy-done, bf16[256,1024]{1,0:T(8,128)(2,1)S(1)} %copy-done.1, ...), custom_call_target="tpu_custom_call" | custom-call | tf_op jit(solution)/shard_map/heads_backward/pallas_call | solution.py:475
  84.5 1.1 %convert_element_type.13 = f32[256,1024]{1,0:T(8,128)} convert(bf16[256,1024]{1,0:T(8,128)(2,1)S(1)} %get-tuple-element.6) | non-fusion elementwise | flops 262144 | bytes 1572864 | tf_op jit(solution)/shard_map/convert_element_type | solution.py:516
  85.6 0.8 convert_element_type.14
  86.5 0.8 convert_element_type.15
Async XLA Ops:
  0.6 0.7 copy-start.4
  1.5 1.0 %copy-start = (bf16[256,1024]{1,0:T(8,128)(2,1)S(1)}, bf16[256,1024]{1,0:T(8,128)(2,1)}, u32[]{:S(2)}) copy-start(bf16[256,1024]{1,0:T(8,128)(2,1)} %q.1) | copy-start | bytes 1572868
  2.6 1.0 %copy-start.1 = (bf16[256,1024]{1,0:T(8,128)(2,1)S(1)}, bf16[256,1024]{1,0:T(8,128)(2,1)}, u32[]{:S(2)}) copy-start(bf16[256,1024]{1,0:T(8,128)(2,1)} %do.1) | copy-start | bytes 1572868
  3.6 0.9 %copy-start.2 = (bf16[64,2048]{1,0:T(8,128)(2,1)S(1)}, bf16[64,2048]{1,0:T(8,128)(2,1)}, u32[]{:S(2)}) copy-start(bf16[64,2048]{1,0:T(8,128)(2,1)} %k.1) | copy-start | bytes 786436
  4.6 0.9 %copy-start.3 = (bf16[64,2048]{1,0:T(8,128)(2,1)S(1)}, bf16[64,2048]{1,0:T(8,128)(2,1)}, u32[]{:S(2)}) copy-start(bf16[64,2048]{1,0:T(8,128)(2,1)} %v.1) | copy-start | bytes 786436

commit v3 on v2

--- a/solution.py
+++ b/solution.py
@@ -22,6 +22,7 @@
 TILE = 256
 MESH = pl.DeviceIdType.MESH
 VMEM_LIMIT = 48 * 1024 * 1024
+FUSED_VMEM_LIMIT = 60 * 1024 * 1024
 
 
 class Place:
@@ -181,7 +182,8 @@
     send_heads(me, q, do, k, v, qh, doh, kh, vh, kv_send, kv_recv, q_send, q_recv)
     for n in range(turn_col.shape[0] // HEAD_SIZE):
         at = slice(n * HEAD_SIZE, (n + 1) * HEAD_SIZE)
-        turn_col[at, :] = jnp.broadcast_to(turn_row[:, at], (HEAD_SIZE, HEAD_SIZE)).T
+        turns = turn_row[:, at].astype(jnp.float32)
+        turn_col[at, :] = jnp.broadcast_to(turns, (HEAD_SIZE, HEAD_SIZE)).T
     share_keys(me, kh, vh, kv_recv, k_send, k_recv)
     owner = 2 * me.pair + me.span // me.held
     q_cols = lanes(2 * (me.span % me.held) + me.core)
@@ -191,24 +193,28 @@
         wait_for(qh.at[i * tok : (i + 1) * tok], q_recv.at[0, i])
         wait_for(doh.at[i * tok : (i + 1) * tok], q_recv.at[1, i])
 
-    def send_queries(i):
-        src = dqh.at[i * tok : (i + 1) * tok, :]
-        mine = (me.span == i) & (owner == me.ka)
-
-        @pl.when(mine)
-        def _():
-            pltpu.make_async_copy(src, dq.at[:, q_cols], dq_recv).start()
-
-        @pl.when(jnp.logical_not(mine))
-        def _():
-            pltpu.make_async_remote_copy(
-                src_ref=src,
-                dst_ref=dq.at[:, q_cols],
-                send_sem=dq_send,
-                recv_sem=dq_recv,
-                device_id=me.at(i, owner),
-                device_id_type=MESH,
-            ).start()
+    def in_turn(batch):
+        return [batch[0] + (me.span + t) % len(batch) for t in range(len(batch))]
+
+    def send_queries(batch):
+        for span in in_turn(batch):
+            src = dqh.at[rows_at(span * tok, tok), :]
+            mine = (me.span == span) & (owner == me.ka)
+
+            @pl.when(mine)
+            def _(src=src):
+                pltpu.make_async_copy(src, dq.at[:, q_cols], dq_recv).start()
+
+            @pl.when(jnp.logical_not(mine))
+            def _(src=src, span=span):
+                pltpu.make_async_remote_copy(
+                    src_ref=src,
+                    dst_ref=dq.at[:, q_cols],
+                    send_sem=dq_send,
+                    recv_sem=dq_recv,
+                    device_id=me.at(span, owner),
+                    device_id_type=MESH,
+                ).start()
 
     def share_grads(j):
         at = slice(j * tok, (j + 1) * tok)
@@ -218,62 +224,62 @@
             def _(ref=ref):
                 to_other_core(me, ref.at[at], got.at[at], x_send, x_recv.at[j]).start()
 
-    def send_grads(j):
-        at = slice(j * tok, (j + 1) * tok)
-        wait_for(got.at[at], x_recv.at[j])
+    def send_grads(batch):
+        for j in batch:
+            wait_for(got.at[j * tok : (j + 1) * tok], x_recv.at[j])
         for core, (own, out) in enumerate(((dkh, dk), (dvh, dv))):
 
             @pl.when(me.core == core)
             def _(own=own, out=out, core=core):
+                at = slice(batch[0] * tok, (batch[-1] + 1) * tok)
                 low[at, :] = (own[at, :] + got[at, :]).astype(jnp.bfloat16)
-                for t in range(ka_count):
-                    ka = (me.ka + t) % ka_count
-                    src = low.at[rows_at(j * tok + ka * piece, piece), :]
-                    dst = out.at[:, head_cols]
-
-                    def remote(src=src, dst=dst, ka=ka):
-                        pltpu.make_async_remote_copy(
-                            src_ref=src,
-                            dst_ref=dst,
-                            send_sem=dkv_send,
-                            recv_sem=dkv_recv.at[core],
-                            device_id=me.at(j, ka),
-                            device_id_type=MESH,
-                        ).start()
-
-                    if t == 0:
-                        pl.when(me.span != j)(remote)
-
-                        @pl.when(me.span == j)
-                        def _(src=src, dst=dst):
-                            pltpu.make_async_copy(src, dst, dkv_recv.at[core]).start()
-                    else:
-                        remote()
+                for span in in_turn(batch):
+                    for t in range(ka_count):
+                        ka = (me.ka + t) % ka_count
+                        src = low.at[rows_at(span * tok + ka * piece, piece), :]
+                        dst = out.at[:, head_cols]
+
+                        def remote(src=src, dst=dst, ka=ka, span=span):
+                            pltpu.make_async_remote_copy(
+                                src_ref=src,
+                                dst_ref=dst,
+                                send_sem=dkv_send,
+                                recv_sem=dkv_recv.at[core],
+                                device_id=me.at(span, ka),
+                                device_id_type=MESH,
+                            ).start()
+
+                        if t == 0:
+                            pl.when(me.span != span)(remote)
+
+                            @pl.when(me.span == span)
+                            def _(src=src, dst=dst):
+                                pltpu.make_async_copy(src, dst, dkv_recv.at[core]).start()
+                        else:
+                            remote()
 
     half = spans // 2
-    order = [spans - 1, *range(half), *range(spans - 2, half - 1, -1)]
-    done = set()
-    shared = []
+    top = spans - 1
+    order = [top, *range(half), *range(top - 1, half - 1, -1)]
+    query_batches = {top: [top], half - 1: list(range(half)), top - 1: [top - 1]}
+    query_batches[half] = list(range(half, top - 1))
+    grad_batches = {0: [top], top - 2: [top - 1]}
+    shares = {top: [top], top - 1: [top - 1], top - 2: [top - 2]}
+    shares[half] = list(range(top - 3, -1, -1))
 
     def after(i):
-        send_queries(i)
-        done.add(i)
-        for j in shared:
-            send_grads(j)
-        shared.clear()
-        for j in range(spans - 1, -1, -1):
-            if j not in started and all(n in done for n in range(j, spans)):
-                share_grads(j)
-                started.add(j)
-                shared.append(j)
-
-    started = set()
+        for j in shares.get(i, []):
+            share_grads(j)
+        if i in query_batches:
+            send_queries(query_batches[i])
+        if i in grad_batches:
+            send_grads(grad_batches[i])
+
     attend(
         me, 0, order, ready, after,
         listed, turn_row, turn_col, qh, doh, kh, vh, dqh, dkh, dvh, kt, s_buf, g_buf,
     )
-    for j in shared:
-        send_grads(j)
+    send_grads(list(range(top - 1)))
     finish_heads(me, qh, doh, kh, kv_send, q_send, k_send, tok, piece)
     wait_for(got, x_send)
     sent = spans * tok
@@ -319,7 +325,7 @@
         ready(i)
         q_i = q[i * TILE : (i + 1) * TILE, :]
         do_i = do[i * TILE : (i + 1) * TILE, :]
-        turn_i = turn_row[:, i * TILE : (i + 1) * TILE]
+        turn_i = turn_row[:, i * TILE : (i + 1) * TILE].astype(jnp.float32)
         last = halo // TILE + i
         first = max(0, last - BACK * BLOCK_POSITIONS // TILE)
         peak = jnp.full((8, TILE), NEG_LARGE, jnp.float32)
@@ -475,7 +481,8 @@
         out = pl.pallas_call(
             functools.partial(fused_kernel, spans, ka_count),
             out_shape=grads,
-            in_specs=[pl.BlockSpec(memory_space=pltpu.SMEM), vmem] + [any_space] * 4,
+            in_specs=[pl.BlockSpec(memory_space=pltpu.SMEM), vmem]
+            + [pl.BlockSpec(memory_space=pltpu.HBM)] * 4,
             out_specs=[any_space] * 3,
             scratch_shapes=[low_rows] * 4
             + [
@@ -502,12 +509,12 @@
                 dma((2,)),
             ],
             compiler_params=pltpu.CompilerParams(
-                collective_id=2, has_side_effects=True, vmem_limit_bytes=VMEM_LIMIT
+                collective_id=2, has_side_effects=True, vmem_limit_bytes=FUSED_VMEM_LIMIT
             ),
             name="heads_backward",
         )(
             listed.reshape(-1),
-            turn_ids.astype(f32)[None, :],
+            turn_ids[None, :],
             queries,
             output_gradient,
             key_states,

time: 87.6 us -> 85.2 us (0.973)
  the two profiles are of different devices: /device:TPU:0 before, /device:TPU:13 now
where the time goes in v3:
time: 85.2 us; the launch traced here: 84.8 us
  Pallas kernels  78.7 us (92%)
  other arithmetic  3.83 us (4%)
  local copies, waits for them, and re-layouts  1.65 us (2%)
    pallas_call x1, Pallas kernels, per_device(): pl.pallas_call(functools.partial(fused_kernel, spans, ka_count), out_shap...  78.7 us
    convert_element_type x3, other arithmetic, per_device(): return tuple((part.astype(f32) for part in out))  3.83 us

profile of v3, /device:TPU:13, one launch (start us, length us, event | category | flops | bytes accessed | tf_op | source)
XLA Modules:
  0.0 84.8 jit_solution(8466090771413751270)
XLA Ops:
  0.6 0.8 copy.9
  1.4 0.7 reshape.9.listed
  2.1 78.7 %heads_backward.1 = (bf16[256,1024]{1,0:T(8,128)(2,1)}, bf16[64,2048]{1,0:T(8,128)(2,1)}, bf16[64,2048]{1,0:T(8,128)(2,1)}) custom-call(s32[448]{0:T(512)} %reshape.9.listed, s32[1,2048]{1,0:T(1,128)} %bitcast.1, bf16[256,1024]{1,0:T(8,128)(2,1)} %q.1, bf16[256,1024]{1,0:T(8,128)(2,1)} %do.1, bf16[64,2048]{1,0:T(8,128)(2,1)} %k.1, bf16[64,2048]{1,0:T(8,128)(2,1)} %v.1), custom_call_target="tpu_custom_call" | custom-call | tf_op jit(solution)/shard_map/heads_backward/pallas_call | solution.py:481
  80.8 0.0 copy-start.1
  80.8 2.2 %convert_element_type.9 = f32[256,1024]{1,0:T(8,128)} convert(bf16[256,1024]{1,0:T(8,128)(2,1)} %get-tuple-element.6) | non-fusion elementwise | flops 262144 | bytes 1572864 | tf_op jit(solution)/shard_map/convert_element_type | solution.py:523
  83.0 0.0 copy-done.1
  83.0 0.0 copy-start
  83.0 0.8 convert_element_type.10
  83.8 0.2 copy-done
  84.0 0.8 convert_element_type.11
Async XLA Ops:
  80.8 2.2 %copy-start.1 = (bf16[64,2048]{1,0:T(8,128)(2,1)S(1)}, bf16[64,2048]{1,0:T(8,128)(2,1)}, u32[]{:S(2)}) copy-start(bf16[64,2048]{1,0:T(8,128)(2,1)} %get-tuple-element.7) | copy-start | bytes 786436
  83.0 1.0 %copy-start = (bf16[64,2048]{1,0:T(8,128)(2,1)S(1)}, bf16[64,2048]{1,0:T(8,128)(2,1)}, u32[]{:S(2)}) copy-start(bf16[64,2048]{1,0:T(8,128)(2,1)} %get-tuple-element.8) | copy-start | bytes 786436

commit v4 on v2

--- a/solution.py
+++ b/solution.py
@@ -22,6 +22,7 @@
 TILE = 256
 MESH = pl.DeviceIdType.MESH
 VMEM_LIMIT = 48 * 1024 * 1024
+FUSED_VMEM_LIMIT = 60 * 1024 * 1024
 
 
 class Place:
@@ -181,19 +182,20 @@
     send_heads(me, q, do, k, v, qh, doh, kh, vh, kv_send, kv_recv, q_send, q_recv)
     for n in range(turn_col.shape[0] // HEAD_SIZE):
         at = slice(n * HEAD_SIZE, (n + 1) * HEAD_SIZE)
-        turn_col[at, :] = jnp.broadcast_to(turn_row[:, at], (HEAD_SIZE, HEAD_SIZE)).T
+        turns = turn_row[:, at].astype(jnp.float32)
+        turn_col[at, :] = jnp.broadcast_to(turns, (HEAD_SIZE, HEAD_SIZE)).T
     share_keys(me, kh, vh, kv_recv, k_send, k_recv)
     owner = 2 * me.pair + me.span // me.held
     q_cols = lanes(2 * (me.span % me.held) + me.core)
     head_cols = lanes(me.head)
 
-    def ready(i):
-        wait_for(qh.at[i * tok : (i + 1) * tok], q_recv.at[0, i])
-        wait_for(doh.at[i * tok : (i + 1) * tok], q_recv.at[1, i])
-
-    def send_queries(i):
-        src = dqh.at[i * tok : (i + 1) * tok, :]
-        mine = (me.span == i) & (owner == me.ka)
+    def ready(span):
+        for which, ref in enumerate((qh, doh)):
+            wait_for(ref.at[rows_at(span * tok, tok), :], q_recv.at[which, span])
+
+    def send_queries(span):
+        src = dqh.at[rows_at(span * tok, tok), :]
+        mine = (me.span == span) & (owner == me.ka)
 
         @pl.when(mine)
         def _():
@@ -206,74 +208,74 @@
                 dst_ref=dq.at[:, q_cols],
                 send_sem=dq_send,
                 recv_sem=dq_recv,
-                device_id=me.at(i, owner),
+                device_id=me.at(span, owner),
                 device_id_type=MESH,
             ).start()
 
-    def share_grads(j):
-        at = slice(j * tok, (j + 1) * tok)
+    tile = attend(me, 0, listed, turn_row, turn_col, qh, doh, kh, vh, dqh, dkh, dvh, kt, s_buf, g_buf)
+
+    def query_step(t, carry):
+        span = (me.span + me.held - t // 2) % me.held
+        span = span + me.held * ((t + me.span // me.held) % 2)
+        ready(span)
+        for i in range(spans):
+            pl.when(span == i)(functools.partial(tile, i))
+        send_queries(span)
+        return carry
+
+    lax.fori_loop(0, spans, query_step, 0)
+
+    def share_step(t, carry):
+        span = (me.span + t) % spans
+        at = rows_at(span * tok, tok)
         for core, ref in enumerate((dvh, dkh)):
 
             @pl.when(me.core == core)
             def _(ref=ref):
-                to_other_core(me, ref.at[at], got.at[at], x_send, x_recv.at[j]).start()
-
-    def send_grads(j):
-        at = slice(j * tok, (j + 1) * tok)
-        wait_for(got.at[at], x_recv.at[j])
+                to_other_core(
+                    me, ref.at[at, :], got.at[at, :], x_send, x_recv.at[span]
+                ).start()
+
+        return carry
+
+    lax.fori_loop(0, spans, share_step, 0)
+
+    def grad_step(t, carry):
+        span = (me.span + t) % spans
+        at = rows_at(span * tok, tok)
+        wait_for(got.at[at, :], x_recv.at[span])
         for core, (own, out) in enumerate(((dkh, dk), (dvh, dv))):
 
             @pl.when(me.core == core)
             def _(own=own, out=out, core=core):
                 low[at, :] = (own[at, :] + got[at, :]).astype(jnp.bfloat16)
-                for t in range(ka_count):
-                    ka = (me.ka + t) % ka_count
-                    src = low.at[rows_at(j * tok + ka * piece, piece), :]
-                    dst = out.at[:, head_cols]
-
-                    def remote(src=src, dst=dst, ka=ka):
+                dst = out.at[:, head_cols]
+                for n in range(ka_count):
+                    ka = (me.ka + n) % ka_count
+                    src = low.at[rows_at(span * tok + ka * piece, piece), :]
+
+                    def remote(src=src, ka=ka):
                         pltpu.make_async_remote_copy(
                             src_ref=src,
                             dst_ref=dst,
                             send_sem=dkv_send,
                             recv_sem=dkv_recv.at[core],
-                            device_id=me.at(j, ka),
+                            device_id=me.at(span, ka),
                             device_id_type=MESH,
                         ).start()
 
-                    if t == 0:
-                        pl.when(me.span != j)(remote)
-
-                        @pl.when(me.span == j)
-                        def _(src=src, dst=dst):
+                    if n == 0:
+                        pl.when(me.span != span)(remote)
+
+                        @pl.when(me.span == span)
+                        def _(src=src):
                             pltpu.make_async_copy(src, dst, dkv_recv.at[core]).start()
                     else:
                         remote()
 
-    half = spans // 2
-    order = [spans - 1, *range(half), *range(spans - 2, half - 1, -1)]
-    done = set()
-    shared = []
-
-    def after(i):
-        send_queries(i)
-        done.add(i)
-        for j in shared:
-            send_grads(j)
-        shared.clear()
-        for j in range(spans - 1, -1, -1):
-            if j not in started and all(n in done for n in range(j, spans)):
-                share_grads(j)
-                started.add(j)
-                shared.append(j)
-
-    started = set()
-    attend(
-        me, 0, order, ready, after,
-        listed, turn_row, turn_col, qh, doh, kh, vh, dqh, dkh, dvh, kt, s_buf, g_buf,
-    )
-    for j in shared:
-        send_grads(j)
+        return carry
+
+    lax.fori_loop(0, spans, grad_step, 0)
     finish_heads(me, qh, doh, kh, kv_send, q_send, k_send, tok, piece)
     wait_for(got, x_send)
     sent = spans * tok
@@ -286,20 +288,16 @@
 
 
 def attention_kernel(spans, ka_count, halo, *refs):
-    order = list(range(refs[3].shape[0] // TILE))
-    nothing = lambda i: None
-    attend(Place(spans, ka_count), halo, order, nothing, nothing, *refs)
-
-
-def attend(
-    me, halo, order, ready, after,
-    listed, turn_row, turn_col, q, do, k, v, dq, dk, dv, kt, s_buf, g_buf,
-):
+    tile = attend(Place(spans, ka_count), halo, *refs)
+    for i in range(refs[3].shape[0] // TILE):
+        tile(i)
+
+
+def attend(me, halo, listed, turn_row, turn_col, q, do, k, v, dq, dk, dv, kt, s_buf, g_buf):
     rows = q.shape[0]
     keys = k.shape[0]
-    blocks = listed.shape[0] // (HEAD_GROUPS * BACK)
     head_group = me.head // (KEY_VALUE_HEADS // HEAD_GROUPS)
-    list_base = (head_group * blocks + me.group * (rows // BLOCK_POSITIONS)) * BACK
+    block_base = me.group * (rows // BLOCK_POSITIONS)
     dk[...] = jnp.zeros_like(dk)
     dv[...] = jnp.zeros_like(dv)
     for n in range(keys // TILE):
@@ -312,14 +310,13 @@
     def hit(block, key_block):
         offset = block - key_block - 1
         if 0 <= offset < BACK:
-            return listed[list_base + block * BACK + offset]
+            return listed[head_group, block_base + block, offset]
         return jnp.int32(0)
 
-    for i in order:
-        ready(i)
+    def tile(i):
         q_i = q[i * TILE : (i + 1) * TILE, :]
         do_i = do[i * TILE : (i + 1) * TILE, :]
-        turn_i = turn_row[:, i * TILE : (i + 1) * TILE]
+        turn_i = turn_row[:, i * TILE : (i + 1) * TILE].astype(jnp.float32)
         last = halo // TILE + i
         first = max(0, last - BACK * BLOCK_POSITIONS // TILE)
         peak = jnp.full((8, TILE), NEG_LARGE, jnp.float32)
@@ -368,7 +365,8 @@
             dk[at, :] += jnp.dot(mixed, q_i, preferred_element_type=jnp.float32)
             dq_t = dq_t + jnp.dot(kt[:, at], mixed, preferred_element_type=jnp.float32)
         dq[i * TILE : (i + 1) * TILE, :] = dq_t.T.astype(jnp.bfloat16)
-        after(i)
+
+    return tile
 
 
 def scatter_kernel(
@@ -475,7 +473,8 @@
         out = pl.pallas_call(
             functools.partial(fused_kernel, spans, ka_count),
             out_shape=grads,
-            in_specs=[pl.BlockSpec(memory_space=pltpu.SMEM), vmem] + [any_space] * 4,
+            in_specs=[pl.BlockSpec(memory_space=pltpu.SMEM), vmem]
+            + [pl.BlockSpec(memory_space=pltpu.HBM)] * 4,
             out_specs=[any_space] * 3,
             scratch_shapes=[low_rows] * 4
             + [
@@ -502,12 +501,12 @@
                 dma((2,)),
             ],
             compiler_params=pltpu.CompilerParams(
-                collective_id=2, has_side_effects=True, vmem_limit_bytes=VMEM_LIMIT
+                collective_id=2, has_side_effects=True, vmem_limit_bytes=FUSED_VMEM_LIMIT
             ),
             name="heads_backward",
         )(
-            listed.reshape(-1),
-            turn_ids.astype(f32)[None, :],
+            listed,
+            turn_ids[None, :],
             queries,
             output_gradient,
             key_states,
@@ -549,7 +548,7 @@
         compiler_params=pltpu.CompilerParams(vmem_limit_bytes=VMEM_LIMIT),
         name="attention_backward",
     )(
-        listed.reshape(-1),
+        listed,
         turn_own.astype(f32)[None, :],
         jnp.broadcast_to(turn_keys.astype(f32)[:, None], (keys, HEAD_SIZE)),
         q,

time: 87.6 us -> 70.6 us (0.81); the launches traced: 87.3 us -> 69.2 us
  Pallas kernels: 79 us -> 63.1 us
  local copies, waits for them, and re-layouts: 4.17 us -> 1.57 us
    pallas_call x1, Pallas kernels: 79 us -> 63.1 us  [per_device(): pl.pallas_call(functools.partial(fused_kernel, spans, ka_count), out_shap...]
    unnamed x11 -> x5, local copies, waits for them, and re-layouts: 4.07 us -> 1.57 us
    convert_element_type x3, other arithmetic: 2.74 us -> 3.83 us  [per_device(): return tuple((part.astype(f32) for part in out))]
where the time goes in v4:
time: 70.6 us; the launch traced here: 69.2 us
  Pallas kernels  63.1 us (89%)
  other arithmetic  3.83 us (5%)
  local copies, waits for them, and re-layouts  1.57 us (2%)
    pallas_call x1, Pallas kernels, per_device(): pl.pallas_call(functools.partial(fused_kernel, spans, ka_count), out_shap...  63.1 us
    convert_element_type x3, other arithmetic, per_device(): return tuple((part.astype(f32) for part in out))  3.83 us
    unnamed x5, local copies, waits for them, and re-layouts  1.57 us

profile of v4, /device:TPU:0, one launch (start us, length us, event | category | flops | bytes accessed | tf_op | source)
XLA Modules:
  0.0 69.2 jit_solution(7175180804280040229)
XLA Ops:
  0.6 1.4 %copy.9.listed = s32[2,16,14]{2,1,0:T(8,128)} copy(s32[2,16,14]{1,0,2:T(2,128)} %param.11) | data formatting | bytes 3584 | tf_op args[5]
  2.0 63.1 %heads_backward.1 = (bf16[256,1024]{1,0:T(8,128)(2,1)}, bf16[64,2048]{1,0:T(8,128)(2,1)}, bf16[64,2048]{1,0:T(8,128)(2,1)}) custom-call(s32[2,16,14]{2,1,0:T(8,128)} %copy.9.listed, s32[1,2048]{1,0:T(1,128)} %bitcast.1, bf16[256,1024]{1,0:T(8,128)(2,1)} %q.1, bf16[256,1024]{1,0:T(8,128)(2,1)} %do.1, bf16[64,2048]{1,0:T(8,128)(2,1)} %k.1, bf16[64,2048]{1,0:T(8,128)(2,1)} %v.1), custom_call_target="tpu_custom_call" | custom-call | tf_op jit(solution)/shard_map/heads_backward/pallas_call | solution.py:473
  65.2 0.0 copy-start.1
  65.2 2.2 %convert_element_type.9 = f32[256,1024]{1,0:T(8,128)} convert(bf16[256,1024]{1,0:T(8,128)(2,1)} %get-tuple-element.6) | non-fusion elementwise | flops 262144 | bytes 1572864 | tf_op jit(solution)/shard_map/convert_element_type | solution.py:515
  67.4 0.0 copy-done.1
  67.4 0.0 copy-start
  67.4 0.8 %convert_element_type.10 = f32[64,2048]{1,0:T(8,128)} convert(bf16[64,2048]{1,0:T(8,128)(2,1)S(1)} %copy-done.1) | non-fusion elementwise | flops 131072 | bytes 786432 | tf_op jit(solution)/shard_map/convert_element_type | solution.py:515
  68.2 0.2 copy-done
  68.4 0.8 %convert_element_type.11 = f32[64,2048]{1,0:T(8,128)} convert(bf16[64,2048]{1,0:T(8,128)(2,1)S(1)} %copy-done) | non-fusion elementwise | flops 131072 | bytes 786432 | tf_op jit(solution)/shard_map/convert_element_type | solution.py:515
Async XLA Ops:
  65.2 2.2 %copy-start.1 = (bf16[64,2048]{1,0:T(8,128)(2,1)S(1)}, bf16[64,2048]{1,0:T(8,128)(2,1)}, u32[]{:S(2)}) copy-start(bf16[64,2048]{1,0:T(8,128)(2,1)} %get-tuple-element.7) | copy-start | bytes 786436
  67.4 1.0 %copy-start = (bf16[64,2048]{1,0:T(8,128)(2,1)S(1)}, bf16[64,2048]{1,0:T(8,128)(2,1)}, u32[]{:S(2)}) copy-start(bf16[64,2048]{1,0:T(8,128)(2,1)} %get-tuple-element.8) | copy-start | bytes 786436

commit v5 on v4

--- a/solution.py
+++ b/solution.py
@@ -310,7 +310,7 @@
     def hit(block, key_block):
         offset = block - key_block - 1
         if 0 <= offset < BACK:
-            return listed[head_group, block_base + block, offset]
+            return listed[offset, head_group, block_base + block]
         return jnp.int32(0)
 
     def tile(i):
@@ -447,6 +447,27 @@
     wait_for(dv, kv_recv.at[1])
 
 
+def widen_kernel(*refs):
+    for src, dst in zip(refs[:3], refs[3:]):
+        dst[...] = src[...].astype(jnp.float32)
+
+
+def widen(parts):
+    steps = 4
+    blocks = [pl.BlockSpec((p.shape[0] // steps, p.shape[1]), lambda i: (i, 0)) for p in parts]
+    return tuple(
+        pl.pallas_call(
+            widen_kernel,
+            grid=(steps,),
+            out_shape=[jax.ShapeDtypeStruct(p.shape, jnp.float32) for p in parts],
+            in_specs=blocks,
+            out_specs=blocks,
+            compiler_params=pltpu.CompilerParams(vmem_limit_bytes=FUSED_VMEM_LIMIT),
+            name="widen_gradients",
+        )(*parts)
+    )
+
+
 def per_device(queries, output_gradient, key_states, value_inputs, turn_ids, listed):
     ka_count = lax.axis_size("ka")
     pb_count = lax.axis_size("pb")
@@ -505,14 +526,14 @@
             ),
             name="heads_backward",
         )(
-            listed,
+            jnp.transpose(listed, (2, 0, 1)),
             turn_ids[None, :],
             queries,
             output_gradient,
             key_states,
             value_inputs,
         )
-        return tuple(part.astype(f32) for part in out)
+        return widen(out)
 
     q, do, k, v = pl.pallas_call(
         functools.partial(gather_kernel, spans, ka_count),
@@ -548,7 +569,7 @@
         compiler_params=pltpu.CompilerParams(vmem_limit_bytes=VMEM_LIMIT),
         name="attention_backward",
     )(
-        listed,
+        jnp.transpose(listed, (2, 0, 1)),
         turn_own.astype(f32)[None, :],
         jnp.broadcast_to(turn_keys.astype(f32)[:, None], (keys, HEAD_SIZE)),
         q,
@@ -581,7 +602,7 @@
         ),
         name="scatter_gradients",
     )(dq, dk, dv)
-    return tuple(part.astype(f32) for part in out)
+    return widen(out)
 
 
 def solution(mesh):

time: 70.6 us -> 68.6 us (0.972)
  other arithmetic: 3.83 us -> 0 us
  Pallas kernels: 63.1 us -> 66.7 us
  local copies, waits for them, and re-layouts: 1.57 us -> 0 us
    convert_element_type x3 -> x0, other arithmetic: 3.83 us -> none  [per_device(): return tuple((part.astype(f32) for part in out))]
    pallas_call x0 -> x1, Pallas kernels: none -> 3.54 us  [widen(): pl.pallas_call(widen_kernel, grid=(steps,), out_shape=[jax.ShapeDtypeStru...]
    unnamed x5 -> x0, local copies, waits for them, and re-layouts: 1.57 us -> none
where the time goes in v5:
time: 68.6 us; the launch traced here: 67.3 us
  Pallas kernels  66.7 us (97%)
    pallas_call x1, Pallas kernels, per_device(): pl.pallas_call(functools.partial(fused_kernel, spans, ka_count), out_shap...  63.1 us
    pallas_call x1, Pallas kernels, widen(): pl.pallas_call(widen_kernel, grid=(steps,), out_shape=[jax.ShapeDtypeStru...  3.54 us

profile of v5, /device:TPU:0, one launch (start us, length us, event | category | flops | bytes accessed | tf_op | source)
XLA Modules:
  0.0 67.3 jit_solution(14481498619175862746)
XLA Ops:
  0.6 63.1 %heads_backward.1 = (bf16[256,1024]{1,0:T(8,128)(2,1)}, bf16[64,2048]{1,0:T(8,128)(2,1)}, bf16[64,2048]{1,0:T(8,128)(2,1)}) custom-call(s32[14,2,16]{2,1,0:T(2,128)} %bitcast.2, s32[1,2048]{1,0:T(1,128)} %bitcast.3, bf16[256,1024]{1,0:T(8,128)(2,1)} %q.1, bf16[256,1024]{1,0:T(8,128)(2,1)} %do.1, bf16[64,2048]{1,0:T(8,128)(2,1)} %k.1, bf16[64,2048]{1,0:T(8,128)(2,1)} %v.1), custom_call_target="tpu_custom_call" | custom-call | tf_op jit(solution)/shard_map/heads_backward/pallas_call | solution.py:494
  63.7 3.5 %widen_gradients.1 = (f32[256,1024]{1,0:T(8,128)}, f32[64,2048]{1,0:T(8,128)}, f32[64,2048]{1,0:T(8,128)}) custom-call(bf16[256,1024]{1,0:T(8,128)(2,1)} %get-tuple-element.6.refs_0_, bf16[64,2048]{1,0:T(8,128)(2,1)} %get-tuple-element.7.refs_1_, bf16[64,2048]{1,0:T(8,128)(2,1)} %get-tuple-element.8.refs_2_), custom_call_target="tpu_custom_call" | custom-call | tf_op jit(solution)/shard_map/widen_gradients/pallas_call | solution.py:459
